TPU v7x, 32 devices: a whole 2x2x4 slice. The times are simulated.
32 devices in a mesh: dp: 4 (over y, core), label: 8 (over z, x).
Axes of the slice: x: 2, y: 2, z: 4, core: 2. Of those that a mesh axis runs over, the one named last changes fastest.
Arguments:
- feats: bfloat16 [2048, 1024], P('dp'), may hold values from -2 to 2
- weights: bfloat16 [128, 256, 1024], P(('dp', 'label')), may hold values from -5 to 5
- shortlist: int32 [16, 16], replicated, may hold values from 0 to 127, as said below
- slot_of: int32 [128], replicated, may hold values from 0 to 127, as said below
- positives: int32 [2048, 8], P('dp'), may hold values from 0 to 32767, as said below
Outputs:
- loss: float32 [2048], P('dp')
- grad_feats: bfloat16 [2048, 1024], P('dp', 'label')
Inputs may be any that keep to these rules, and one draw needn't show every extreme that they name: `slot_of`: A permutation of the cluster ids: the slot of each cluster. For each index d of dp, its blocks d * 4 to d * 4 + 3: the first 2 of them together shortlist one cluster stored on each device (the device of slot s being s // 4 in the order of the weights' placement), each once, and the last 2 shortlist the same clusters, each once; so every such cluster is shortlisted by exactly two blocks of d. `positives`: an instance's 8 labels are different, and each lies in a cluster that the instance's block shortlists.
All inputs are finite; a program needn't handle non-finite values.
Results may differ from a plain program's by a relative error of at most 0.0034.
Values may be sent and summed in bfloat16 or wider, within the bound.
No kernel may reach another device: no remote copies, remote signals or barrier semaphores. Data moves between devices by JAX's collectives and lax.ppermute only.
A program may use at most 64 MiB of HBM per device.

v0:
```python
import functools

import jax
import jax.numpy as jnp
from jax import lax
from jax.experimental import pallas as pl
from jax.experimental.pallas import tpu as pltpu
from jax.sharding import PartitionSpec as P

BLK = 128
NEG_FILL = -1e30
VMEM_BYTES = 32 * 1024 * 1024
VMEM_PICK = 56 * 1024 * 1024


def divide(value, by):
    if by & (by - 1) == 0:
        return lax.shift_right_logical(value, jnp.int32(by.bit_length() - 1))
    return lax.div(value, jnp.int32(by))


def remainder(value, by):
    if by & (by - 1) == 0:
        return value & jnp.int32(by - 1)
    return lax.rem(value, jnp.int32(by))


def each_entry(count, short_count, body, carry):
    if count <= 64:
        for e in range(count):
            carry = body(e // short_count, e % short_count, carry)
        return carry
    step = lambda e, c: body(divide(e, short_count), remainder(e, short_count), c)
    return lax.fori_loop(0, count, step, carry)


class Plan:
    def __init__(self, square, dp_count, lab_count, stored, block_count, short_count):
        self.square, self.dp_count, self.lab_count = square, dp_count, lab_count
        self.stored, self.block_count, self.short_count = stored, block_count, short_count

    def here(self):
        return lax.axis_index("dp"), lax.axis_index("label")

    def home(self):
        dp, lab = self.here()
        return (dp & ~1) | (lab & 1) if self.square else dp

    def flips(self, entry, core):
        return [(0, 0), (1, 1), (core, 1 - core), (1 - core, core)][entry]

    def wanted_by(self, entry):
        dp, lab = self.here()
        if not self.square:
            return dp ^ entry
        flip_x, flip_y = self.flips(entry, dp & 1)
        return ((dp >> 1) ^ flip_y) * 2 + ((lab & 1) ^ flip_x)

    def entry_of(self, device):
        dp, lab = self.here()
        that_dp, that_lab = divide(device, self.lab_count), remainder(device, self.lab_count)
        if not self.square:
            return that_lab == lab, that_dp ^ dp
        match = ((that_dp & 1) == (dp & 1)) & ((that_lab >> 1) == (lab >> 1))
        flip_y, flip_x = (that_dp ^ dp) >> 1, (that_lab ^ lab) & 1
        core = dp & 1
        lone = jnp.where(flip_y == 1 - core, 2, 3)
        entry = jnp.where(flip_x + flip_y == 1, lone, (flip_x + flip_y) >> 1)
        return match, entry

    def pairs(self, entry):
        result = []
        for dp in range(self.dp_count):
            for lab in range(self.lab_count):
                if self.square:
                    flip_x, flip_y = self.flips(entry, dp & 1)
                    target = (dp ^ (2 * flip_y)) * self.lab_count + (lab ^ flip_x)
                else:
                    target = (dp ^ entry) * self.lab_count + lab
                result.append((dp * self.lab_count + lab, target))
        return result


def find_slots(plan, wanted, lists_ref, slot_ref):
    dp_index, lab_index = plan.here()
    mine = dp_index * plan.lab_count + lab_index
    stored, short_count = plan.stored, plan.short_count
    found = []
    for k in wanted:
        base = plan.wanted_by(k) * plan.block_count

        def look(row, column, slot_here, base=base):
            slot = slot_ref[lists_ref[base + row, column]]
            return jnp.where(divide(slot, stored) == mine, remainder(slot, stored), slot_here)

        count = plan.block_count // 2 * short_count
        found.append(each_entry(count, short_count, look, jnp.int32(0)))
    return found


def far_kernel(plan, wanted, lists_hbm, slot_hbm, weights_ref, *rest):
    outs = rest[: len(wanted)]
    held, lists_ref, slot_ref, sems = rest[len(wanted) :]
    tables = [
        pltpu.make_async_copy(lists_hbm, lists_ref, sems.at[0]),
        pltpu.make_async_copy(slot_hbm, slot_ref, sems.at[1]),
    ]
    stage = pltpu.make_async_copy(weights_ref, held, sems.at[2])
    for copy in tables:
        copy.start()
    stage.start()
    for copy in tables:
        copy.wait()
    found = find_slots(plan, wanted, lists_ref, slot_ref)
    stage.wait()
    copies = []
    for i, slot in enumerate(found):
        copies.append(pltpu.make_async_copy(held.at[slot], outs[i], sems.at[3 + i]))
        copies[-1].start()
    for copy in copies:
        copy.wait()


def near_kernel(plan, lists_ref, slot_ref, weights_ref, table_ref, *rest):
    block_count, short_count = plan.block_count, plan.short_count
    outs, sems = rest[:-1], rest[-1]
    copies = []
    for k, slot in enumerate(find_slots(plan, range(1), lists_ref, slot_ref)):
        copies.append(pltpu.make_async_copy(weights_ref.at[slot], outs[k], sems.at[k]))
        copies[-1].start()
    home = plan.home()
    half = block_count // 2
    for side in range(2):

        def note(row, column, carry, side=side):
            block = side * half + row
            cluster = lists_ref[home * block_count + block, column]
            match, entry = plan.entry_of(divide(slot_ref[cluster], plan.stored))

            @pl.when(match)
            def _():
                table_ref[entry, 0] = cluster
                table_ref[entry, 1 + side] = jnp.int32(block)

            return carry

        each_entry(half * short_count, short_count, note, jnp.int32(0))
    for copy in copies:
        copy.wait()


def home_kernel(feats_ref, pos_ref, other_feats_ref, other_pos_ref, home_feats_ref, home_pos_ref):
    same = (lax.axis_index("dp") & 1) == (lax.axis_index("label") & 1)

    @pl.when(same)
    def _():
        home_feats_ref[...] = feats_ref[...]
        home_pos_ref[...] = pos_ref[...]

    @pl.when(jnp.logical_not(same))
    def _():
        home_feats_ref[...] = other_feats_ref[...]
        home_pos_ref[...] = other_pos_ref[...]


def target_kernel(early, late, table_ref, pos_ref, feats_ref, hits_ref, shares_ref, turned_ref):
    count, cluster_size, _ = hits_ref.shape
    pos_count = pos_ref.shape[1]

    def one_slot(s):
        labels = lax.broadcasted_iota(jnp.int32, (cluster_size, BLK), 0) + table_ref[s, 0] * cluster_size
        for side in range(2):
            pos = pos_ref[table_ref[s, 1 + side]]
            hit = pos[0:1, :] == labels
            for p in range(1, pos_count):
                hit = hit | (pos[p : p + 1, :] == labels)
            hits = jnp.where(hit, 1.0, 0.0)
            columns = pl.ds(side * BLK, BLK)
            hits_ref[s, :, columns] = hits
            if s in early:
                shares_ref[early.index(s), columns, :] = (hits / pos_count).T
            else:
                feats = feats_ref[table_ref[s, 1 + side]].astype(jnp.float32)
                turned_ref[late.index(s), :, columns] = feats.T.astype(jnp.bfloat16)

    for s in range(count):
        pl.when(table_ref[s, 0] >= 0)(functools.partial(one_slot, s))


def logit_kernel(slots, turned, copies, table_ref, feats_ref, hits_ref, *rest):
    count = len(slots)
    rows = rest[:count]
    logits_ref, out_ref, stats_ref = rest[-3:]
    if len(rest) == count + 3:
        stats_ref[0] = jnp.full(stats_ref.shape[1:], NEG_FILL, jnp.float32)
        stats_ref[1] = jnp.zeros(stats_ref.shape[1:], jnp.float32)
        stats_ref[2] = jnp.zeros(stats_ref.shape[1:], jnp.float32)
    else:
        stats_ref[...] = rest[count][0]
    for i, (s, ref) in enumerate(zip(slots, rows)):
        if not turned:
            logits_ref[i] = jnp.dot(ref[...], feats_ref[i], preferred_element_type=jnp.float32)
        for side in range(2):
            block = table_ref[s, 1 + side]
            columns = pl.ds(side * BLK, BLK)
            if turned:
                logits = lax.dot_general(
                    ref[...],
                    feats_ref[block],
                    (((1,), (1,)), ((), ())),
                    preferred_element_type=jnp.float32,
                )
                logits_ref[i, columns, :] = logits.T
            else:
                logits = logits_ref[i, :, columns]
            highest = jnp.max(logits, axis=0, keepdims=True)
            total = jnp.sum(jnp.exp(logits - highest), axis=0, keepdims=True)
            positive = jnp.sum(hits_ref[s, :, columns] * logits, axis=0, keepdims=True)
            row = pl.ds(block, 1)
            before = stats_ref[0, row, :]
            after = jnp.maximum(before, highest)
            stats_ref[0, row, :] = after
            stats_ref[1, row, :] = stats_ref[1, row, :] * jnp.exp(before - after) + total * jnp.exp(
                highest - after
            )
            stats_ref[2, row, :] = stats_ref[2, row, :] + positive
    for i in range(copies):
        out_ref[i] = stats_ref[...]


def row_sums(stats_ref, lab_count):
    highest = stats_ref[0, 0]
    for i in range(1, lab_count):
        highest = jnp.maximum(highest, stats_ref[i, 0])
    summed = jnp.zeros_like(highest)
    positive = jnp.zeros_like(highest)
    for i in range(lab_count):
        summed = summed + stats_ref[i, 1] * jnp.exp(stats_ref[i, 0] - highest)
        positive = positive + stats_ref[i, 2]
    return highest + jnp.log(summed), positive


def prepare(stats_ref, pos_count, lab_count, loss_ref, lse_ref, columns_ref, total_ref, first):
    lse, positive = row_sums(stats_ref, lab_count)
    lse_ref[...] = lse
    loss_ref[...] = lse - positive / pos_count
    for b in range(columns_ref.shape[0]):
        columns_ref[b] = jnp.broadcast_to(lse[first + b : first + b + 1, :], (BLK, BLK)).T
    total_ref[...] = jnp.zeros_like(total_ref)


def add_slots(sides, groups, pos_count, first, table_ref, hits_ref, shares_ref, logits_refs, rows, sums):
    lse_ref, columns_ref, total_ref = sums
    early = [s for slots in groups[:-1] for s in slots]
    cluster_size = rows[0].shape[0]

    def one_slot(s, logits_ref):
        for side in sides:
            block = table_ref[s, 1 + side]
            here = pl.ds(side * BLK, BLK)
            if s in early:
                column = columns_ref[block - first]
                column = jnp.concatenate([column] * (cluster_size // BLK), axis=1)
                dlogit = jnp.exp(logits_ref[here, :] - column) - shares_ref[early.index(s), here, :]
            else:
                row = lse_ref[pl.ds(block, 1), :]
                dlogit = jnp.exp(logits_ref[:, here] - row) - hits_ref[s, :, here] / pos_count
                dlogit = dlogit.T
            total_ref[block - first] += lax.dot_general(
                dlogit.astype(jnp.bfloat16),
                rows[s][...],
                (((1,), (0,)), ((), ())),
                preferred_element_type=jnp.float32,
            )

    for slots, logits_ref in zip(groups, logits_refs):
        for i, s in enumerate(slots):
            body = functools.partial(one_slot, s, logits_ref.at[i])
            if len(rows) <= 4:
                body()
            else:
                pl.when(table_ref[s, 0] >= 0)(body)


def half_kernel(side, groups, lab_count, pos_count, table_ref, hits_ref, shares_ref, stats_ref, *rest):
    logits_refs = rest[: len(groups)]
    rows = rest[len(groups) : -6]
    loss_ref, keep_ref, send_ref, lse_ref, columns_ref, total_ref = rest[-6:]
    half = total_ref.shape[0]
    prepare(
        stats_ref, pos_count, lab_count, loss_ref, lse_ref, columns_ref, total_ref, side * half
    )
    add_slots(
        (side,),
        groups,
        pos_count,
        side * half,
        table_ref,
        hits_ref,
        shares_ref,
        logits_refs,
        rows,
        (lse_ref, columns_ref, total_ref),
    )
    part = keep_ref.shape[2]
    core, line = lax.axis_index("dp") & 1, lax.axis_index("label") >> 1
    for j in range(lab_count // 2):
        first = (line ^ j) * 2
        mine = pl.ds(pl.multiple_of((first + 1 - core) * part, part), part)
        other = pl.ds(pl.multiple_of((first + core) * part, part), part)
        for b in range(half):
            here = pl.ds(b * BLK, BLK)
            keep_ref[j, here, :] = total_ref[b, :, mine]
            send_ref[j, here, :] = total_ref[b, :, other].astype(jnp.bfloat16)


def pair_kernel(keep_ref, got_ref, next_ref, send_ref):
    for j in range(keep_ref.shape[0]):
        total = keep_ref[j] + got_ref[j].astype(jnp.float32)
        out_ref = send_ref if j % 2 else next_ref
        out_ref[j // 2] = total.astype(out_ref.dtype)


def spread_kernel(keep_ref, got_ref, *outs):
    for j, out_ref in enumerate(outs):
        out_ref[...] = (keep_ref[j] + got_ref[j].astype(jnp.float32)).astype(out_ref.dtype)


def step_kernel(keep_ref, got_ref, own_ref, send_ref):
    own_ref[...] = keep_ref[0] + got_ref[0].astype(jnp.float32)
    send_ref[...] = (keep_ref[1] + got_ref[1].astype(jnp.float32)).astype(jnp.bfloat16)


def line_kernel(*refs):
    total = refs[0][...]
    for ref in refs[1:-1]:
        total = total + ref[...].astype(jnp.float32)
    refs[-1][...] = total.astype(jnp.bfloat16)


def line_and_loss_kernel(loss_ref, *refs):
    out_ref, terms_ref = refs[-2:]
    rows = refs[0].shape[0]
    line_kernel(*refs[:-2], out_ref.at[:rows, :])
    terms_ref[...] = jnp.zeros_like(terms_ref)
    blocks = loss_ref.shape[0]
    rest = loss_ref[...]
    for i in range(3):
        term = rest.astype(jnp.bfloat16).astype(jnp.float32)
        terms_ref[i * blocks : (i + 1) * blocks, :] = term
        rest = rest - term
    out_ref[rows:, :] = terms_ref[...].astype(jnp.bfloat16)


def home_again_kernel(low_ref, high_ref, loss_ref, grads_ref):
    blocks = loss_ref.shape[0]
    rows = high_ref.shape[0]
    grads_ref[:rows, :] = low_ref[:rows, :]
    grads_ref[rows:, :] = high_ref[...]
    terms = low_ref[rows:, :].astype(jnp.float32)
    loss_ref[...] = terms[:blocks] + (terms[blocks : 2 * blocks] + terms[2 * blocks : 3 * blocks])


def grad_kernel(groups, lab_count, pos_count, table_ref, hits_ref, shares_ref, stats_ref, *rest):
    logits_refs = rest[: len(groups)]
    rows = rest[len(groups) : -5]
    loss_ref, out_ref, lse_ref, columns_ref, total_ref = rest[-5:]
    prepare(stats_ref, pos_count, lab_count, loss_ref, lse_ref, columns_ref, total_ref, 0)
    add_slots(
        (0, 1),
        groups,
        pos_count,
        0,
        table_ref,
        hits_ref,
        shares_ref,
        logits_refs,
        rows,
        (lse_ref, columns_ref, total_ref),
    )
    part = out_ref.shape[2]
    for j in range(lab_count):
        for b in range(total_ref.shape[0]):
            out_ref[j, b * BLK : (b + 1) * BLK, :] = total_ref[
                b, :, j * part : (j + 1) * part
            ].astype(jnp.bfloat16)


def smem():
    return pl.BlockSpec(memory_space=pltpu.SMEM)


def vmem():
    return pl.BlockSpec(memory_space=pltpu.VMEM)


def anywhere():
    return pl.BlockSpec(memory_space=pl.ANY)


def call(kernel, name, out_shape, in_specs, arrays, scratch=(), limit=VMEM_BYTES, out_specs=None):
    return pl.pallas_call(
        kernel,
        out_shape=out_shape,
        in_specs=in_specs,
        out_specs=out_specs or [vmem()] * len(out_shape),
        scratch_shapes=list(scratch),
        compiler_params=pltpu.CompilerParams(vmem_limit_bytes=limit),
        name=name,
    )(*arrays)


def shards(feats, weights, shortlist, slot_of, positives):
    dp_count = lax.axis_size("dp")
    lab_count = lax.axis_size("label")
    stored, cluster_size, width = weights.shape
    inst_count = feats.shape[0]
    pos_count = positives.shape[1]
    block_count = inst_count // BLK
    part = width // lab_count
    square = dp_count == 4 and lab_count == 8 and part % 128 == 0
    plan = Plan(square, dp_count, lab_count, stored, block_count, shortlist.shape[1])
    struct = jax.ShapeDtypeStruct
    row_type = struct((cluster_size, width), weights.dtype)
    stat_shape = (3, block_count, BLK)
    both = ("dp", "label")
    devices = [(dp, lab) for dp in range(dp_count) for lab in range(lab_count)]

    def move(x, target):
        pairs = []
        for dp, lab in devices:
            to_dp, to_lab = target(dp, lab)
            pairs.append((dp * lab_count + lab, to_dp * lab_count + to_lab))
        return lax.ppermute(x, both, pairs)

    feat_blocks = feats.reshape(block_count, BLK, width)
    pos_blocks = positives.reshape(block_count, BLK, pos_count).transpose(0, 2, 1)
    if square:
        other_feats = lax.ppermute(feat_blocks, "dp", [(i, i ^ 1) for i in range(dp_count)])
        other_pos = lax.ppermute(pos_blocks, "dp", [(i, i ^ 1) for i in range(dp_count)])
        feat_blocks, pos_blocks = call(
            home_kernel,
            "home",
            [struct(feat_blocks.shape, feats.dtype), struct(pos_blocks.shape, jnp.int32)],
            [vmem()] * 4,
            (feat_blocks, pos_blocks, other_feats, other_pos),
        )

    far = range(1, dp_count)
    far_rows = call(
        functools.partial(far_kernel, plan, far),
        "pick_far",
        [row_type] * len(far),
        [anywhere()] * 3,
        (shortlist, slot_of, weights),
        scratch=[
            pltpu.VMEM(weights.shape, weights.dtype),
            pltpu.SMEM(shortlist.shape, jnp.int32),
            pltpu.SMEM(slot_of.shape, jnp.int32),
            pltpu.SemaphoreType.DMA((3 + len(far),)),
        ],
        limit=VMEM_PICK,
        out_specs=[anywhere()] * len(far),
    )
    table, *rows = call(
        functools.partial(near_kernel, plan),
        "pick_near",
        [struct((dp_count, 4), jnp.int32), row_type],
        [smem(), smem(), anywhere()],
        (shortlist, slot_of, weights),
        scratch=[pltpu.SemaphoreType.DMA((1,))],
        out_specs=[smem(), vmem()],
    )
    for k, x in zip(far, far_rows):
        if square and k == 3:
            x, rows[1] = lax.optimization_barrier((x, rows[1]))
        rows.append(lax.ppermute(x, both, plan.pairs(k)))

    if square:
        groups = [(0,), (1,), (2,), (3,)]
    else:
        cuts = (0, dp_count // 2, dp_count * 3 // 4, dp_count)
        groups = [tuple(range(a, b)) for a, b in zip(cuts[:-1], cuts[1:])]
    early = [s for slots in groups[:-1] for s in slots]
    late = list(groups[-1])
    hits, shares, turned = call(
        functools.partial(target_kernel, early, late),
        "targets",
        [
            struct((dp_count, cluster_size, 2 * BLK), jnp.float32),
            struct((len(early), 2 * BLK, cluster_size), jnp.float32),
            struct((len(late), width, 2 * BLK), feats.dtype),
        ],
        [smem()] + [vmem()] * 2,
        (table, pos_blocks, feat_blocks),
    )
    kept = []
    stats = []
    for slots in groups:
        last = slots is groups[-1]
        copies = lab_count if last else 1
        shape = (cluster_size, 2 * BLK) if last else (2 * BLK, cluster_size)
        logits, stats_out = call(
            functools.partial(logit_kernel, slots, not last, copies),
            "logits",
            [
                struct((len(slots),) + shape, jnp.float32),
                struct((copies,) + stat_shape, jnp.float32),
            ],
            [smem()] + [vmem()] * (2 + len(slots) + len(stats)),
            (table, turned if last else feat_blocks, hits, *[rows[s] for s in slots], *stats),
            scratch=[pltpu.VMEM(stat_shape, jnp.float32)],
        )
        kept.append(logits)
        stats = [stats_out]

    in_specs = [smem()] + [vmem()] * (3 + len(groups) + dp_count)
    loss_type = struct((block_count, BLK), jnp.float32)
    lse_scratch = pltpu.VMEM((block_count, BLK), jnp.float32)
    if not square:
        all_stats = lax.all_to_all(stats[0], "label", split_axis=0, concat_axis=0, tiled=True)
        loss, parts = call(
            functools.partial(grad_kernel, groups, lab_count, pos_count),
            "grads",
            [loss_type, struct((lab_count, inst_count, part), jnp.bfloat16)],
            in_specs,
            (table, hits, shares, all_stats, *kept, *rows),
            scratch=[
                lse_scratch,
                pltpu.VMEM((block_count, BLK, BLK), jnp.float32),
                pltpu.VMEM((block_count, BLK, width), jnp.float32),
            ],
        )
        gathered = lax.all_to_all(parts, "label", split_axis=0, concat_axis=0, tiled=True)
        grads = jnp.sum(gathered.astype(jnp.float32), axis=0).astype(jnp.bfloat16)
        return loss.reshape(inst_count), grads

    owners = [
        [(2 * y + core) * lab_count + 2 * z + x for z in range(lab_count // 2) for core in range(2)]
        for y in range(dp_count // 2)
        for x in range(2)
    ]
    all_stats = lax.all_to_all(
        stats[0], both, split_axis=0, concat_axis=0, axis_index_groups=owners, tiled=True
    )
    pairs = lab_count // 2
    half_rows = inst_count // 2
    wide = struct((half_rows, part), jnp.float32)
    narrow = struct((half_rows, part), jnp.bfloat16)

    halves = []
    for side in range(2):
        loss, keep, send = call(
            functools.partial(half_kernel, side, groups, lab_count, pos_count),
            "grads",
            [
                loss_type,
                struct((pairs, half_rows, part), jnp.float32),
                struct((pairs, half_rows, part), jnp.bfloat16),
            ],
            in_specs,
            (table, hits, shares, all_stats, *kept, *rows),
            scratch=[
                lse_scratch,
                pltpu.VMEM((block_count // 2, BLK, BLK), jnp.float32),
                pltpu.VMEM((block_count // 2, BLK, width), jnp.float32),
            ],
        )
        halves.append((keep, lax.ppermute(send, "dp", [(i, i ^ 1) for i in range(dp_count)])))

    def hop(x, mask):
        return lax.ppermute(x, "label", [(i, i ^ mask) for i in range(lab_count)])

    keep, send = call(
        pair_kernel,
        "pair_sums",
        [struct((2, half_rows, part), jnp.float32), struct((2, half_rows, part), jnp.bfloat16)],
        [vmem()] * 2,
        halves[1],
    )
    got = hop(send, 2)
    spread = call(
        spread_kernel, "spread_sums", [wide] + [narrow] * (pairs - 1), [vmem()] * 2, halves[0]
    )
    low = [spread[0]] + [hop(x, 2 * j + 2) for j, x in enumerate(spread[1:])]
    got, *_ = lax.optimization_barrier((got, *spread))
    own, send = call(step_kernel, "step_sums", [wide, narrow], [vmem()] * 2, (keep, got))
    high = [own, hop(send, 4)]
    extra = -(-3 * block_count // 16) * 16

    def deliver(x):
        return move(x, lambda dp, lab: ((dp & ~1) | (lab & 1), (lab & ~1) | (1 - (dp & 1))))

    (low,) = call(
        line_and_loss_kernel,
        "line_sums_loss",
        [struct((half_rows + extra, part), jnp.bfloat16)],
        [vmem()] * (1 + len(low)),
        (loss, *low),
        scratch=[pltpu.VMEM((extra, part), jnp.float32)],
    )
    low_home = deliver(low)
    *high, low = lax.optimization_barrier((*high, low))
    (high,) = call(line_kernel, "line_sums", [narrow], [vmem()] * 2, high)
    loss, grads = call(
        home_again_kernel,
        "home_again",
        [loss_type, struct((inst_count, part), jnp.bfloat16)],
        [vmem()] * 2,
        (low_home, deliver(high)),
    )
    return loss.reshape(inst_count), grads


def solution(mesh):
    in_specs = (P("dp", None), P(("dp", "label"), None, None), P(), P(), P("dp", None))
    out_specs = (P("dp"), P("dp", "label"))
    return jax.shard_map(shards, mesh=mesh, in_specs=in_specs, out_specs=out_specs, check_vma=False)
```

profile of v0, /device:TPU:0, one launch (start us, length us, event | category | flops | bytes accessed | tf_op | source)
XLA Modules:
  0.0 65.4 jit_solution(5538841490362826925)
XLA Ops:
  0.6 0.0 copy-start
  0.6 0.0 copy-start.2
  0.7 0.0 copy-start.4
  0.7 0.0 copy-start.1
  0.7 0.0 copy-start.3
  0.7 0.5 collective-permute-start
  1.2 3.1 %pick_far.1 = (bf16[256,1024]{1,0:T(8,128)(2,1)}, bf16[256,1024]{1,0:T(8,128)(2,1)}, bf16[256,1024]{1,0:T(8,128)(2,1)}) custom-call(s32[16,16]{1,0:T(8,128)} %lists_hbm.1, s32[128]{0:T(128)} %slot_hbm.1, bf16[4,256,1024]{2,1,0:T(8,128)(2,1)} %weights_ref.3), custom_call_target="tpu_custom_call" | custom-call | tf_op jit(solution)/shard_map/pick_far/pallas_call | solution.py:402
  4.3 3.4 %collective-permute-start.2 = (bf16[256,1024]{1,0:T(8,128)(2,1)}, bf16[256,1024]{1,0:T(8,128)(2,1)S(1)}, u32[]{:S(2)}, u32[]{:S(2)}) collective-permute-start(bf16[256,1024]{1,0:T(8,128)(2,1)} %get-tuple-element.47), channel_id=1, source_target_pairs={{0,17},{1,16},{2,19},{3,18},{4,21},{5,20},{6,23},{7,22},{8,25},{9,... | collective-permute-start | bytes 1572872 | tf_op jit(solution)/shard_map/ppermute | solution.py:477
  7.7 0.5 collective-permute-start.4
  8.2 12.5 %collective-permute-done.2.rest_0_.rest_5_ = bf16[256,1024]{1,0:T(8,128)(2,1)S(1)} collective-permute-done((bf16[256,1024]{1,0:T(8,128)(2,1)}, bf16[256,1024]{1,0:T(8,128)(2,1)S(1)}, u32[]{:S(2)}, u32[]{:S(2)}) %collective-permute-start.2) | collective-permute-done | bytes 524320 | tf_op jit(solution)/shard_map/ppermute | solution.py:477
  20.7 1.9 %collective-permute-start.3 = (bf16[256,1024]{1,0:T(8,128)(2,1)}, bf16[256,1024]{1,0:T(8,128)(2,1)S(1)}, u32[]{:S(2)}, u32[]{:S(2)}) collective-permute-start(bf16[256,1024]{1,0:T(8,128)(2,1)} %get-tuple-element.48), channel_id=1, source_target_pairs={{0,1},{1,0},{2,3},{3,2},{4,5},{5,4},{6,7},{7,6},{8,24},{9,25},{10,... | collective-permute-start | bytes 1572872 | tf_op jit(solution)/shard_map/ppermute | solution.py:477
  22.6 0.0 collective-permute-start.1
  22.6 0.0 copy-done.2
  22.6 0.0 copy-done.4
  22.6 1.9 %pick_near.1 = (s32[4,4]{1,0:T(4,128)S(1)}, bf16[256,1024]{1,0:T(8,128)(2,1)S(1)}) custom-call(s32[16,16]{1,0:T(8,128)S(1)} %copy-done.2, s32[128]{0:T(128)S(1)} %copy-done.4, bf16[4,256,1024]{2,1,0:T(8,128)(2,1)S(1)} %copy-done), custom_call_target="tpu_custom_call" | custom-call | tf_op jit(solution)/shard_map/pick_near/pallas_call | solution.py:402
  24.5 0.0 collective-permute-done.1.other_pos_ref
  24.5 0.0 collective-permute-done.other_feats_ref
  24.6 0.1 home.1
  24.7 1.9 %targets.1 = (f32[4,256,256]{2,1,0:T(8,128)S(1)}, f32[3,256,256]{2,1,0:T(8,128)S(1)}, bf16[1,1024,256]{2,1,0:T(8,128)(2,1)S(1)}) custom-call(s32[4,4]{1,0:T(4,128)S(1)} %get-tuple-element.40.table_ref, s32[4,8,128]{2,1,0:T(8,128)S(1)} %get-tuple-element.41.pos_ref, bf16[4,128,1024]{2,1,0:T(8,128)(2,1)S(1)} %get-tuple-element.42.feats_ref), custom_call_target="tpu_custom_call" | custom-call | tf_op jit(solution)/shard_map/targets/pallas_call | solution.py:402
  26.6 1.1 %logits.4 = (f32[1,256,256]{2,1,0:T(8,128)S(1)}, f32[1,3,4,128]{3,2,1,0:T(4,128)S(1)}) custom-call(s32[4,4]{1,0:T(4,128)S(1)} %get-tuple-element.40.table_ref, bf16[4,128,1024]{2,1,0:T(8,128)(2,1)S(1)} %get-tuple-element.42.feats_ref, f32[4,256,256]{2,1,0:T(8,128)S(1)} %get-tuple-element.43.hits_ref, bf16[256,1024]{1,0:T(8,128)(2,1)S(1)} %get-tuple-element.51.rest_0_.rest_4_), custom_call_target="tpu_custom_call" | custom-call | tf_op jit(solution)/shard_map/logits/pallas_call | solution.py:402
  27.7 1.1 %logits.5 = (f32[1,256,256]{2,1,0:T(8,128)S(1)}, f32[1,3,4,128]{3,2,1,0:T(4,128)S(1)}) custom-call(s32[4,4]{1,0:T(4,128)S(1)} %get-tuple-element.40.table_ref, bf16[4,128,1024]{2,1,0:T(8,128)(2,1)S(1)} %get-tuple-element.42.feats_ref, f32[4,256,256]{2,1,0:T(8,128)S(1)} %get-tuple-element.43.hits_ref, ...), custom_call_target="tpu_custom_call" | custom-call | tf_op jit(solution)/shard_map/logits/pallas_call | solution.py:402
  28.9 0.1 collective-permute-done.4.rest_0_.rest_6_
  28.9 1.1 %logits.6 = (f32[1,256,256]{2,1,0:T(8,128)S(1)}, f32[1,3,4,128]{3,2,1,0:T(4,128)S(1)}) custom-call(s32[4,4]{1,0:T(4,128)S(1)} %get-tuple-element.40.table_ref, bf16[4,128,1024]{2,1,0:T(8,128)(2,1)S(1)} %get-tuple-element.42.feats_ref, f32[4,256,256]{2,1,0:T(8,128)S(1)} %get-tuple-element.43.hits_ref, ...), custom_call_target="tpu_custom_call" | custom-call | tf_op jit(solution)/shard_map/logits/pallas_call | solution.py:402
  30.0 2.1 %collective-permute-done.3.rest_0_.rest_7_ = bf16[256,1024]{1,0:T(8,128)(2,1)S(1)} collective-permute-done((bf16[256,1024]{1,0:T(8,128)(2,1)}, bf16[256,1024]{1,0:T(8,128)(2,1)S(1)}, u32[]{:S(2)}, u32[]{:S(2)}) %collective-permute-start.3) | collective-permute-done | bytes 524320 | tf_op jit(solution)/shard_map/ppermute | solution.py:477
  32.1 0.9 %logits.7 = (f32[1,256,256]{2,1,0:T(8,128)S(1)}, f32[8,3,4,128]{3,2,1,0:T(4,128)S(1)}) custom-call(s32[4,4]{1,0:T(4,128)S(1)} %get-tuple-element.40.table_ref, bf16[1,1024,256]{2,1,0:T(8,128)(2,1)S(1)} %get-tuple-element.45.feats_ref, f32[4,256,256]{2,1,0:T(8,128)S(1)} %get-tuple-element.43.hits_ref, ...), custom_call_target="tpu_custom_call" | custom-call | tf_op jit(solution)/shard_map/logits/pallas_call | solution.py:402
  33.0 10.5 %all_to_all.5.stats_ref = f32[8,3,4,128]{3,2,1,0:T(4,128)S(1)} all-to-all(f32[8,3,4,128]{3,2,1,0:T(4,128)S(1)} %get-tuple-element.55), channel_id=1, replica_groups={{0,8,2,10,4,12,6,14},{1,9,3,11,5,13,7,15},{16,24,18,26,20,28,22,30},{17..., dimensions={0} | all-to-all | bytes 98304 | tf_op jit(solution)/shard_map/all_to_all | solution.py:543
  43.5 1.4 %grads.2 = (f32[4,128]{1,0:T(4,128)S(1)}, f32[4,256,128]{2,1,0:T(8,128)S(1)}, bf16[4,256,128]{2,1,0:T(8,128)(2,1)S(1)}) custom-call(s32[4,4]{1,0:T(4,128)S(1)} %get-tuple-element.40.table_ref, f32[4,256,256]{2,1,0:T(8,128)S(1)} %get-tuple-element.43.hits_ref, f32[3,256,256]{2,1,0:T(8,128)S(1)} %get-tuple-element.44.shares_ref, ...), custom_call_target="tpu_custom_call" | custom-call | tf_op jit(solution)/shard_map/grads/pallas_call | solution.py:402
  44.9 0.1 collective-permute-start.10
  45.0 1.8 %grads.3 = (f32[4,128]{1,0:T(4,128)}, f32[4,256,128]{2,1,0:T(8,128)S(1)}, bf16[4,256,128]{2,1,0:T(8,128)(2,1)S(1)}) custom-call(s32[4,4]{1,0:T(4,128)S(1)} %get-tuple-element.40.table_ref, f32[4,256,256]{2,1,0:T(8,128)S(1)} %get-tuple-element.43.hits_ref, f32[3,256,256]{2,1,0:T(8,128)S(1)} %get-tuple-element.44.shares_ref, ...), custom_call_target="tpu_custom_call" | custom-call | tf_op jit(solution)/shard_map/grads/pallas_call | solution.py:402
  46.8 0.5 collective-permute-start.5
  47.3 0.0 collective-permute-done.10.got_ref
  47.4 0.8 %collective-permute-start.11 = (bf16[2,256,128]{2,1,0:T(8,128)(2,1)S(1)}, bf16[2,256,128]{2,1,0:T(8,128)(2,1)S(1)}, u32[]{:S(2)}, u32[]{:S(2)}) collective-permute-start(bf16[2,256,128]{2,1,0:T(8,128)(2,1)S(1)} %get-tuple-element.70), channel_id=1, source_target_pairs={{0,2},{1,3},{2,0},{3,1},{4,6},{5,7},{6,4},{7,5},{8,10},{9,11},{10,... | collective-permute-start | bytes 393224 | tf_op jit(solution)/shard_map/ppermute | solution.py:572
  48.1 0.4 collective-permute-done.5.got_ref
  48.5 0.1 spread_sums.1
  48.6 1.1 %collective-permute-start.6 = (bf16[256,128]{1,0:T(8,128)(2,1)S(1)}, bf16[256,128]{1,0:T(8,128)(2,1)S(1)}, u32[]{:S(2)}, u32[]{:S(2)}) collective-permute-start(bf16[256,128]{1,0:T(8,128)(2,1)S(1)} %get-tuple-element.64), channel_id=1, source_target_pairs={{0,2},{1,3},{2,0},{3,1},{4,6},{5,7},{6,4},{7,5},{8,10},{9,11},{10,... | collective-permute-start | bytes 196616 | tf_op jit(solution)/shard_map/ppermute | solution.py:572
  49.6 0.5 collective-permute-start.7
  50.1 2.9 %collective-permute-start.8 = (bf16[256,128]{1,0:T(8,128)(2,1)S(1)}, bf16[256,128]{1,0:T(8,128)(2,1)S(1)}, u32[]{:S(2)}, u32[]{:S(2)}) collective-permute-start(bf16[256,128]{1,0:T(8,128)(2,1)S(1)} %get-tuple-element.66), channel_id=1, source_target_pairs={{0,6},{1,7},{2,4},{3,5},{4,2},{5,3},{6,0},{7,1},{8,14},{9,15},{10,... | collective-permute-start | bytes 196616 | tf_op jit(solution)/shard_map/ppermute | solution.py:572
  53.0 1.3 %collective-permute-done.11.got_ref = bf16[2,256,128]{2,1,0:T(8,128)(2,1)S(1)} collective-permute-done((bf16[2,256,128]{2,1,0:T(8,128)(2,1)S(1)}, bf16[2,256,128]{2,1,0:T(8,128)(2,1)S(1)}, u32[]{:S(2)}, u32[]{:S(2)}) %collective-permute-start.11) | collective-permute-done | bytes 131104 | tf_op jit(solution)/shard_map/ppermute | solution.py:572
  54.4 0.1 collective-permute-start.12
  54.4 0.7 %collective-permute-done.6.refs_1_ = bf16[256,128]{1,0:T(8,128)(2,1)S(1)} collective-permute-done((bf16[256,128]{1,0:T(8,128)(2,1)S(1)}, bf16[256,128]{1,0:T(8,128)(2,1)S(1)}, u32[]{:S(2)}, u32[]{:S(2)}) %collective-permute-start.6) | collective-permute-done | bytes 65568 | tf_op jit(solution)/shard_map/ppermute | solution.py:572
  55.2 4.4 %collective-permute-done.7.refs_2_ = bf16[256,128]{1,0:T(8,128)(2,1)S(1)} collective-permute-done((bf16[256,128]{1,0:T(8,128)(2,1)S(1)}, bf16[256,128]{1,0:T(8,128)(2,1)S(1)}, u32[]{:S(2)}, u32[]{:S(2)}) %collective-permute-start.7) | collective-permute-done | bytes 65568 | tf_op jit(solution)/shard_map/ppermute | solution.py:572
  59.5 0.0 collective-permute-done.8.refs_3_
  59.6 1.5 %collective-permute-start.9 = (bf16[272,128]{1,0:T(8,128)(2,1)S(1)}, bf16[272,128]{1,0:T(8,128)(2,1)S(1)}, u32[]{:S(2)}, u32[]{:S(2)}) collective-permute-start(bf16[272,128]{1,0:T(8,128)(2,1)S(1)} %line_sums_loss.1), channel_id=1, source_target_pairs={{0,1},{1,9},{2,3},{3,11},{4,5},{5,13},{6,7},{7,15},{8,0},{9,8},{10... | collective-permute-start | bytes 208904 | tf_op jit(solution)/shard_map/ppermute | solution.py:434
  61.1 0.2 collective-permute-done.12.refs_1_
  61.4 1.5 %collective-permute-start.13 = (bf16[256,128]{1,0:T(8,128)(2,1)S(1)}, bf16[256,128]{1,0:T(8,128)(2,1)S(1)}, u32[]{:S(2)}, u32[]{:S(2)}) collective-permute-start(bf16[256,128]{1,0:T(8,128)(2,1)S(1)} %line_sums.1), channel_id=1, source_target_pairs={{0,1},{1,9},{2,3},{3,11},{4,5},{5,13},{6,7},{7,15},{8,0},{9,8},{10... | collective-permute-start | bytes 196616 | tf_op jit(solution)/shard_map/ppermute | solution.py:434
  62.9 0.2 collective-permute-done.9.low_ref
  63.0 1.7 %collective-permute-done.13.high_ref = bf16[256,128]{1,0:T(8,128)(2,1)S(1)} collective-permute-done((bf16[256,128]{1,0:T(8,128)(2,1)S(1)}, bf16[256,128]{1,0:T(8,128)(2,1)S(1)}, u32[]{:S(2)}, u32[]{:S(2)}) %collective-permute-start.13) | collective-permute-done | bytes 65568 | tf_op jit(solution)/shard_map/ppermute | solution.py:434
  64.8 0.7 %home_again.1 = (f32[4,128]{1,0:T(4,128)}, bf16[512,128]{1,0:T(8,128)(2,1)}) custom-call(bf16[272,128]{1,0:T(8,128)(2,1)S(1)} %collective-permute-done.9.low_ref, bf16[256,128]{1,0:T(8,128)(2,1)S(1)} %collective-permute-done.13.high_ref), custom_call_target="tpu_custom_call" | custom-call | tf_op jit(solution)/shard_map/home_again/pallas_call | solution.py:402
  (7 shorter events, 0.1 us)
Async XLA Ops:
  0.6 22.0 %copy-start = (bf16[4,256,1024]{2,1,0:T(8,128)(2,1)S(1)}, bf16[4,256,1024]{2,1,0:T(8,128)(2,1)}, u32[]{:S(2)}) copy-start(bf16[4,256,1024]{2,1,0:T(8,128)(2,1)} %weights_ref.3) | copy-start | bytes 6291460
  0.6 22.0 %copy-start.2 = (s32[16,16]{1,0:T(8,128)S(1)}, s32[16,16]{1,0:T(8,128)}, u32[]{:S(2)}) copy-start(s32[16,16]{1,0:T(8,128)} %lists_hbm.1) | copy-start | bytes 3076
  0.7 22.0 %copy-start.4 = (s32[128]{0:T(128)S(1)}, s32[128]{0:T(128)}, u32[]{:S(2)}) copy-start(s32[128]{0:T(128)} %slot_hbm.1) | copy-start | bytes 1540
  0.7 23.9 %copy-start.1 = (bf16[512,1024]{1,0:T(8,128)(2,1)S(1)}, bf16[512,1024]{1,0:T(8,128)(2,1)}, u32[]{:S(2)}) copy-start(bf16[512,1024]{1,0:T(8,128)(2,1)} %param.5) | copy-start | bytes 3145732
  0.7 23.9 %copy-start.3 = (s32[512,8]{0,1:T(8,128)S(1)}, s32[512,8]{0,1:T(8,128)}, u32[]{:S(2)}) copy-start(s32[512,8]{0,1:T(8,128)} %param.9) | copy-start | bytes 49156
  0.7 23.9 %collective-permute-start = (bf16[4,128,1024]{2,1,0:T(8,128)(2,1)}, bf16[4,128,1024]{2,1,0:T(8,128)(2,1)S(1)}, u32[]{:S(2)}, u32[]{:S(2)}) collective-permute-start(bf16[4,128,1024]{2,1,0:T(8,128)(2,1)} %bitcast.5), channel_id=1, source_target_pairs={{0,8},{8,0},{16,24},{24,16},{1,9},{9,1},{17,25},{25,17},{2,10},{10... | collective-permute-start | bytes 3145736 | tf_op jit(solution)/shard_map/ppermute | solution.py:439
  4.3 16.4 %collective-permute-start.2 = (bf16[256,1024]{1,0:T(8,128)(2,1)}, bf16[256,1024]{1,0:T(8,128)(2,1)S(1)}, u32[]{:S(2)}, u32[]{:S(2)}) collective-permute-start(bf16[256,1024]{1,0:T(8,128)(2,1)} %get-tuple-element.47), channel_id=1, source_target_pairs={{0,17},{1,16},{2,19},{3,18},{4,21},{5,20},{6,23},{7,22},{8,25},{9,... | collective-permute-start | bytes 1572872 | tf_op jit(solution)/shard_map/ppermute | solution.py:477
  7.7 21.2 %collective-permute-start.4 = (bf16[256,1024]{1,0:T(8,128)(2,1)}, bf16[256,1024]{1,0:T(8,128)(2,1)S(1)}, u32[]{:S(2)}, u32[]{:S(2)}) collective-permute-start(bf16[256,1024]{1,0:T(8,128)(2,1)} %get-tuple-element.49), channel_id=1, source_target_pairs={{0,16},{1,17},{2,18},{3,19},{4,20},{5,21},{6,22},{7,23},{8,9},{9,8... | collective-permute-start | bytes 1572872 | tf_op jit(solution)/shard_map/ppermute | solution.py:477
  20.7 11.3 %collective-permute-start.3 = (bf16[256,1024]{1,0:T(8,128)(2,1)}, bf16[256,1024]{1,0:T(8,128)(2,1)S(1)}, u32[]{:S(2)}, u32[]{:S(2)}) collective-permute-start(bf16[256,1024]{1,0:T(8,128)(2,1)} %get-tuple-element.48), channel_id=1, source_target_pairs={{0,1},{1,0},{2,3},{3,2},{4,5},{5,4},{6,7},{7,6},{8,24},{9,25},{10,... | collective-permute-start | bytes 1572872 | tf_op jit(solution)/shard_map/ppermute | solution.py:477
  22.6 1.9 %collective-permute-start.1 = (s32[4,8,128]{2,1,0:T(8,128)}, s32[4,8,128]{2,1,0:T(8,128)S(1)}, u32[]{:S(2)}, u32[]{:S(2)}) collective-permute-start(s32[4,8,128]{2,1,0:T(8,128)} %bitcast.7), channel_id=1, source_target_pairs={{0,8},{8,0},{16,24},{24,16},{1,9},{9,1},{17,25},{25,17},{2,10},{10... | collective-permute-start | bytes 49160 | tf_op jit(solution)/shard_map/ppermute | solution.py:440
  44.9 2.4 %collective-permute-start.10 = (bf16[4,256,128]{2,1,0:T(8,128)(2,1)S(1)}, bf16[4,256,128]{2,1,0:T(8,128)(2,1)S(1)}, u32[]{:S(2)}, u32[]{:S(2)}) collective-permute-start(bf16[4,256,128]{2,1,0:T(8,128)(2,1)S(1)} %get-tuple-element.68), channel_id=1, source_target_pairs={{0,8},{8,0},{16,24},{24,16},{1,9},{9,1},{17,25},{25,17},{2,10},{10... | collective-permute-start | bytes 786440 | tf_op jit(solution)/shard_map/ppermute | solution.py:569
  46.8 1.7 %collective-permute-start.5 = (bf16[4,256,128]{2,1,0:T(8,128)(2,1)S(1)}, bf16[4,256,128]{2,1,0:T(8,128)(2,1)S(1)}, u32[]{:S(2)}, u32[]{:S(2)}) collective-permute-start(bf16[4,256,128]{2,1,0:T(8,128)(2,1)S(1)} %get-tuple-element.62), channel_id=1, source_target_pairs={{0,8},{8,0},{16,24},{24,16},{1,9},{9,1},{17,25},{25,17},{2,10},{10... | collective-permute-start | bytes 786440 | tf_op jit(solution)/shard_map/ppermute | solution.py:569
  47.4 6.9 %collective-permute-start.11 = (bf16[2,256,128]{2,1,0:T(8,128)(2,1)S(1)}, bf16[2,256,128]{2,1,0:T(8,128)(2,1)S(1)}, u32[]{:S(2)}, u32[]{:S(2)}) collective-permute-start(bf16[2,256,128]{2,1,0:T(8,128)(2,1)S(1)} %get-tuple-element.70), channel_id=1, source_target_pairs={{0,2},{1,3},{2,0},{3,1},{4,6},{5,7},{6,4},{7,5},{8,10},{9,11},{10,... | collective-permute-start | bytes 393224 | tf_op jit(solution)/shard_map/ppermute | solution.py:572
  48.6 6.6 %collective-permute-start.6 = (bf16[256,128]{1,0:T(8,128)(2,1)S(1)}, bf16[256,128]{1,0:T(8,128)(2,1)S(1)}, u32[]{:S(2)}, u32[]{:S(2)}) collective-permute-start(bf16[256,128]{1,0:T(8,128)(2,1)S(1)} %get-tuple-element.64), channel_id=1, source_target_pairs={{0,2},{1,3},{2,0},{3,1},{4,6},{5,7},{6,4},{7,5},{8,10},{9,11},{10,... | collective-permute-start | bytes 196616 | tf_op jit(solution)/shard_map/ppermute | solution.py:572
  49.6 9.9 %collective-permute-start.7 = (bf16[256,128]{1,0:T(8,128)(2,1)S(1)}, bf16[256,128]{1,0:T(8,128)(2,1)S(1)}, u32[]{:S(2)}, u32[]{:S(2)}) collective-permute-start(bf16[256,128]{1,0:T(8,128)(2,1)S(1)} %get-tuple-element.65), channel_id=1, source_target_pairs={{0,4},{1,5},{2,6},{3,7},{4,0},{5,1},{6,2},{7,3},{8,12},{9,13},{10,... | collective-permute-start | bytes 196616 | tf_op jit(solution)/shard_map/ppermute | solution.py:572
  50.1 9.4 %collective-permute-start.8 = (bf16[256,128]{1,0:T(8,128)(2,1)S(1)}, bf16[256,128]{1,0:T(8,128)(2,1)S(1)}, u32[]{:S(2)}, u32[]{:S(2)}) collective-permute-start(bf16[256,128]{1,0:T(8,128)(2,1)S(1)} %get-tuple-element.66), channel_id=1, source_target_pairs={{0,6},{1,7},{2,4},{3,5},{4,2},{5,3},{6,0},{7,1},{8,14},{9,15},{10,... | collective-permute-start | bytes 196616 | tf_op jit(solution)/shard_map/ppermute | solution.py:572
  54.4 7.0 %collective-permute-start.12 = (bf16[256,128]{1,0:T(8,128)(2,1)S(1)}, bf16[256,128]{1,0:T(8,128)(2,1)S(1)}, u32[]{:S(2)}, u32[]{:S(2)}) collective-permute-start(bf16[256,128]{1,0:T(8,128)(2,1)S(1)} %get-tuple-element.73), channel_id=1, source_target_pairs={{0,4},{1,5},{2,6},{3,7},{4,0},{5,1},{6,2},{7,3},{8,12},{9,13},{10,... | collective-permute-start | bytes 196616 | tf_op jit(solution)/shard_map/ppermute | solution.py:572
  59.6 3.4 %collective-permute-start.9 = (bf16[272,128]{1,0:T(8,128)(2,1)S(1)}, bf16[272,128]{1,0:T(8,128)(2,1)S(1)}, u32[]{:S(2)}, u32[]{:S(2)}) collective-permute-start(bf16[272,128]{1,0:T(8,128)(2,1)S(1)} %line_sums_loss.1), channel_id=1, source_target_pairs={{0,1},{1,9},{2,3},{3,11},{4,5},{5,13},{6,7},{7,15},{8,0},{9,8},{10... | collective-permute-start | bytes 208904 | tf_op jit(solution)/shard_map/ppermute | solution.py:434
  61.4 3.4 %collective-permute-start.13 = (bf16[256,128]{1,0:T(8,128)(2,1)S(1)}, bf16[256,128]{1,0:T(8,128)(2,1)S(1)}, u32[]{:S(2)}, u32[]{:S(2)}) collective-permute-start(bf16[256,128]{1,0:T(8,128)(2,1)S(1)} %line_sums.1), channel_id=1, source_target_pairs={{0,1},{1,9},{2,3},{3,11},{4,5},{5,13},{6,7},{7,15},{8,0},{9,8},{10... | collective-permute-start | bytes 196616 | tf_op jit(solution)/shard_map/ppermute | solution.py:434
where the time goes:
time: 65.6 us; the launch traced here: 65.4 us
  waiting for transfers between devices  23.6 us (36%)
  Pallas kernels  15.4 us (23%)
  starting transfers between devices  15.1 us (23%)
  blocking collectives  10.5 us (16%)
  between operations  0.8 us (1%)
    pallas_call x16, Pallas kernels, call(): pl.pallas_call(kernel, out_shape=out_shape, in_specs=in_specs, out_specs=...  15.4 us
    ppermute x3, waiting for transfers between devices, shards(): rows.append(lax.ppermute(x, both, plan.pairs(k)))  14.6 us
    all_to_all x1, blocking collectives, shards(): lax.all_to_all(stats[0], both, split_axis=0, concat_axis=0, axis_index_gr...  10.5 us
    ppermute x5, waiting for transfers between devices, hop(): return lax.ppermute(x, 'label', [(i, i ^ mask) for i in range(lab_count)])  6.64 us
    ppermute x3, starting transfers between devices, shards(): rows.append(lax.ppermute(x, both, plan.pairs(k)))  5.75 us
    ppermute x5, starting transfers between devices, hop(): return lax.ppermute(x, 'label', [(i, i ^ mask) for i in range(lab_count)])  5.3 us
    ppermute x2, starting transfers between devices, move(): return lax.ppermute(x, both, pairs)  3.01 us
    ppermute x2, waiting for transfers between devices, move(): return lax.ppermute(x, both, pairs)  1.91 us
  transfers between devices with their start and end apart: 14, of which 10 were waited for; matrix products, arithmetic and copies ran while one was open for 0% of the time, Pallas kernels for 19%

commit v1 on v0

--- a/solution.py
+++ b/solution.py
@@ -447,21 +447,23 @@
         )
 
     far = range(1, dp_count)
-    far_rows = call(
-        functools.partial(far_kernel, plan, far),
-        "pick_far",
-        [row_type] * len(far),
-        [anywhere()] * 3,
-        (shortlist, slot_of, weights),
-        scratch=[
-            pltpu.VMEM(weights.shape, weights.dtype),
-            pltpu.SMEM(shortlist.shape, jnp.int32),
-            pltpu.SMEM(slot_of.shape, jnp.int32),
-            pltpu.SemaphoreType.DMA((3 + len(far),)),
-        ],
-        limit=VMEM_PICK,
-        out_specs=[anywhere()] * len(far),
-    )
+    far_rows = []
+    for some in (far[:1], far[1:]) if square else (far,):
+        far_rows += call(
+            functools.partial(far_kernel, plan, some),
+            "pick_far",
+            [row_type] * len(some),
+            [anywhere()] * 3,
+            (shortlist, slot_of, weights),
+            scratch=[
+                pltpu.VMEM(weights.shape, weights.dtype),
+                pltpu.SMEM(shortlist.shape, jnp.int32),
+                pltpu.SMEM(slot_of.shape, jnp.int32),
+                pltpu.SemaphoreType.DMA((3 + len(some),)),
+            ],
+            limit=VMEM_PICK,
+            out_specs=[anywhere()] * len(some),
+        )
     table, *rows = call(
         functools.partial(near_kernel, plan),
         "pick_near",

time: 65.6 us -> 65 us (level)
  waiting for transfers between devices: 23.6 us -> 20.6 us
  Pallas kernels: 15.4 us -> 17.4 us
    ppermute x3, waiting for transfers between devices: 14.6 us -> 11.7 us  [shards(): rows.append(lax.ppermute(x, both, plan.pairs(k)))]
    pallas_call x16 -> x17, Pallas kernels: 15.4 us -> 17.4 us  [call(): pl.pallas_call(kernel, out_shape=out_shape, in_specs=in_specs, out_specs=...]
  transfers between devices with their start and end apart: 14 -> 14, of which waited for: 10 -> 9; matrix products, arithmetic and copies ran while one was open for 0% -> 0% of each run, Pallas kernels for 19% -> 22%
where the time goes in v1:
time: 65 us; the launch traced here: 64.8 us
  waiting for transfers between devices  20.6 us (32%)
  Pallas kernels  17.4 us (27%)
  starting transfers between devices  15.4 us (24%)
  blocking collectives  10.5 us (16%)
  between operations  0.81 us (1%)
    pallas_call x17, Pallas kernels, call(): pl.pallas_call(kernel, out_shape=out_shape, in_specs=in_specs, out_specs=...  17.4 us
    ppermute x3, waiting for transfers between devices, shards(): rows.append(lax.ppermute(x, both, plan.pairs(k)))  11.7 us
    all_to_all x1, blocking collectives, shards(): lax.all_to_all(stats[0], both, split_axis=0, concat_axis=0, axis_index_gr...  10.5 us
    ppermute x5, waiting for transfers between devices, hop(): return lax.ppermute(x, 'label', [(i, i ^ mask) for i in range(lab_count)])  6.64 us
    ppermute x3, starting transfers between devices, shards(): rows.append(lax.ppermute(x, both, plan.pairs(k)))  6.05 us
    ppermute x5, starting transfers between devices, hop(): return lax.ppermute(x, 'label', [(i, i ^ mask) for i in range(lab_count)])  5.3 us
    ppermute x2, starting transfers between devices, move(): return lax.ppermute(x, both, pairs)  3 us
    ppermute x2, waiting for transfers between devices, move(): return lax.ppermute(x, both, pairs)  1.91 us
  transfers between devices with their start and end apart: 14, of which 9 were waited for; matrix products, arithmetic and copies ran while one was open for 0% of the time, Pallas kernels for 22%

profile of v1, /device:TPU:0, one launch (start us, length us, event | category | flops | bytes accessed | tf_op | source)
XLA Modules:
  0.0 64.8 jit_solution(12729366716179285506)
XLA Ops:
  0.6 0.0 copy-start
  0.7 0.0 copy-start.2
  0.7 0.0 copy-start.4
  0.7 0.5 collective-permute-start
  1.2 2.5 %pick_far.3 = bf16[256,1024]{1,0:T(8,128)(2,1)} custom-call(s32[16,16]{1,0:T(8,128)} %lists_hbm.3, s32[128]{0:T(128)} %slot_hbm.3, bf16[4,256,1024]{2,1,0:T(8,128)(2,1)} %weights_ref.5), custom_call_target="tpu_custom_call" | custom-call | tf_op jit(solution)/shard_map/pick_far/pallas_call | solution.py:402
  3.7 0.0 copy-start.1
  3.8 3.6 %collective-permute-start.2 = (bf16[256,1024]{1,0:T(8,128)(2,1)}, bf16[256,1024]{1,0:T(8,128)(2,1)S(1)}, u32[]{:S(2)}, u32[]{:S(2)}) collective-permute-start(bf16[256,1024]{1,0:T(8,128)(2,1)} %pick_far.3), channel_id=1, source_target_pairs={{0,17},{1,16},{2,19},{3,18},{4,21},{5,20},{6,23},{7,22},{8,25},{9,... | collective-permute-start | bytes 1572872 | tf_op jit(solution)/shard_map/ppermute | solution.py:479
  7.3 2.6 %pick_far.2 = (bf16[256,1024]{1,0:T(8,128)(2,1)}, bf16[256,1024]{1,0:T(8,128)(2,1)}) custom-call(s32[16,16]{1,0:T(8,128)} %lists_hbm.3, s32[128]{0:T(128)} %slot_hbm.3, bf16[4,256,1024]{2,1,0:T(8,128)(2,1)} %weights_ref.5), custom_call_target="tpu_custom_call" | custom-call | tf_op jit(solution)/shard_map/pick_far/pallas_call | solution.py:402
  9.9 0.6 collective-permute-start.4
  10.5 9.8 %collective-permute-done.2.rest_0_.rest_5_ = bf16[256,1024]{1,0:T(8,128)(2,1)S(1)} collective-permute-done((bf16[256,1024]{1,0:T(8,128)(2,1)}, bf16[256,1024]{1,0:T(8,128)(2,1)S(1)}, u32[]{:S(2)}, u32[]{:S(2)}) %collective-permute-start.2) | collective-permute-done | bytes 524320 | tf_op jit(solution)/shard_map/ppermute | solution.py:479
  20.3 1.9 %collective-permute-start.3 = (bf16[256,1024]{1,0:T(8,128)(2,1)}, bf16[256,1024]{1,0:T(8,128)(2,1)S(1)}, u32[]{:S(2)}, u32[]{:S(2)}) collective-permute-start(bf16[256,1024]{1,0:T(8,128)(2,1)} %get-tuple-element.46), channel_id=1, source_target_pairs={{0,1},{1,0},{2,3},{3,2},{4,5},{5,4},{6,7},{7,6},{8,24},{9,25},{10,... | collective-permute-start | bytes 1572872 | tf_op jit(solution)/shard_map/ppermute | solution.py:479
  22.3 0.0 copy-done.3
  22.3 0.0 collective-permute-start.1
  22.3 1.9 %pick_near.1 = (s32[4,4]{1,0:T(4,128)S(1)}, bf16[256,1024]{1,0:T(8,128)(2,1)S(1)}) custom-call(s32[16,16]{1,0:T(8,128)S(1)} %copy-done.2, s32[128]{0:T(128)S(1)} %copy-done.4, bf16[4,256,1024]{2,1,0:T(8,128)(2,1)S(1)} %copy-done), custom_call_target="tpu_custom_call" | custom-call | tf_op jit(solution)/shard_map/pick_near/pallas_call | solution.py:402
  24.2 0.0 collective-permute-done.1.other_pos_ref
  24.2 0.0 collective-permute-done.other_feats_ref
  24.2 0.0 copy-done.1
  24.2 0.1 home.1
  24.3 1.9 %targets.1 = (f32[4,256,256]{2,1,0:T(8,128)S(1)}, f32[3,256,256]{2,1,0:T(8,128)S(1)}, bf16[1,1024,256]{2,1,0:T(8,128)(2,1)S(1)}) custom-call(s32[4,4]{1,0:T(4,128)S(1)} %get-tuple-element.39.table_ref, s32[4,8,128]{2,1,0:T(8,128)S(1)} %get-tuple-element.40.pos_ref, bf16[4,128,1024]{2,1,0:T(8,128)(2,1)S(1)} %get-tuple-element.41.feats_ref), custom_call_target="tpu_custom_call" | custom-call | tf_op jit(solution)/shard_map/targets/pallas_call | solution.py:402
  26.3 1.1 %logits.4 = (f32[1,256,256]{2,1,0:T(8,128)S(1)}, f32[1,3,4,128]{3,2,1,0:T(4,128)S(1)}) custom-call(s32[4,4]{1,0:T(4,128)S(1)} %get-tuple-element.39.table_ref, bf16[4,128,1024]{2,1,0:T(8,128)(2,1)S(1)} %get-tuple-element.41.feats_ref, f32[4,256,256]{2,1,0:T(8,128)S(1)} %get-tuple-element.42.hits_ref, bf16[256,1024]{1,0:T(8,128)(2,1)S(1)} %get-tuple-element.49.rest_0_.rest_4_), custom_call_target="tpu_custom_call" | custom-call | tf_op jit(solution)/shard_map/logits/pallas_call | solution.py:402
  27.4 1.1 %logits.5 = (f32[1,256,256]{2,1,0:T(8,128)S(1)}, f32[1,3,4,128]{3,2,1,0:T(4,128)S(1)}) custom-call(s32[4,4]{1,0:T(4,128)S(1)} %get-tuple-element.39.table_ref, bf16[4,128,1024]{2,1,0:T(8,128)(2,1)S(1)} %get-tuple-element.41.feats_ref, f32[4,256,256]{2,1,0:T(8,128)S(1)} %get-tuple-element.42.hits_ref, ...), custom_call_target="tpu_custom_call" | custom-call | tf_op jit(solution)/shard_map/logits/pallas_call | solution.py:402
  28.5 0.0 collective-permute-done.4.rest_0_.rest_6_
  28.5 1.1 %logits.6 = (f32[1,256,256]{2,1,0:T(8,128)S(1)}, f32[1,3,4,128]{3,2,1,0:T(4,128)S(1)}) custom-call(s32[4,4]{1,0:T(4,128)S(1)} %get-tuple-element.39.table_ref, bf16[4,128,1024]{2,1,0:T(8,128)(2,1)S(1)} %get-tuple-element.41.feats_ref, f32[4,256,256]{2,1,0:T(8,128)S(1)} %get-tuple-element.42.hits_ref, ...), custom_call_target="tpu_custom_call" | custom-call | tf_op jit(solution)/shard_map/logits/pallas_call | solution.py:402
  29.6 1.9 %collective-permute-done.3.rest_0_.rest_7_ = bf16[256,1024]{1,0:T(8,128)(2,1)S(1)} collective-permute-done((bf16[256,1024]{1,0:T(8,128)(2,1)}, bf16[256,1024]{1,0:T(8,128)(2,1)S(1)}, u32[]{:S(2)}, u32[]{:S(2)}) %collective-permute-start.3) | collective-permute-done | bytes 524320 | tf_op jit(solution)/shard_map/ppermute | solution.py:479
  31.5 1.0 %logits.7 = (f32[1,256,256]{2,1,0:T(8,128)S(1)}, f32[8,3,4,128]{3,2,1,0:T(4,128)S(1)}) custom-call(s32[4,4]{1,0:T(4,128)S(1)} %get-tuple-element.39.table_ref, bf16[1,1024,256]{2,1,0:T(8,128)(2,1)S(1)} %get-tuple-element.44.feats_ref, f32[4,256,256]{2,1,0:T(8,128)S(1)} %get-tuple-element.42.hits_ref, ...), custom_call_target="tpu_custom_call" | custom-call | tf_op jit(solution)/shard_map/logits/pallas_call | solution.py:402
  32.4 10.5 %all_to_all.5.stats_ref = f32[8,3,4,128]{3,2,1,0:T(4,128)S(1)} all-to-all(f32[8,3,4,128]{3,2,1,0:T(4,128)S(1)} %get-tuple-element.53), channel_id=1, replica_groups={{0,8,2,10,4,12,6,14},{1,9,3,11,5,13,7,15},{16,24,18,26,20,28,22,30},{17..., dimensions={0} | all-to-all | bytes 98304 | tf_op jit(solution)/shard_map/all_to_all | solution.py:545
  43.0 1.4 %grads.2 = (f32[4,128]{1,0:T(4,128)S(1)}, f32[4,256,128]{2,1,0:T(8,128)S(1)}, bf16[4,256,128]{2,1,0:T(8,128)(2,1)S(1)}) custom-call(s32[4,4]{1,0:T(4,128)S(1)} %get-tuple-element.39.table_ref, f32[4,256,256]{2,1,0:T(8,128)S(1)} %get-tuple-element.42.hits_ref, f32[3,256,256]{2,1,0:T(8,128)S(1)} %get-tuple-element.43.shares_ref, ...), custom_call_target="tpu_custom_call" | custom-call | tf_op jit(solution)/shard_map/grads/pallas_call | solution.py:402
  44.3 0.1 collective-permute-start.10
  44.4 1.8 %grads.3 = (f32[4,128]{1,0:T(4,128)}, f32[4,256,128]{2,1,0:T(8,128)S(1)}, bf16[4,256,128]{2,1,0:T(8,128)(2,1)S(1)}) custom-call(s32[4,4]{1,0:T(4,128)S(1)} %get-tuple-element.39.table_ref, f32[4,256,256]{2,1,0:T(8,128)S(1)} %get-tuple-element.42.hits_ref, f32[3,256,256]{2,1,0:T(8,128)S(1)} %get-tuple-element.43.shares_ref, ...), custom_call_target="tpu_custom_call" | custom-call | tf_op jit(solution)/shard_map/grads/pallas_call | solution.py:402
  46.2 0.5 collective-permute-start.5
  46.7 0.0 collective-permute-done.10.got_ref
  46.8 0.8 %collective-permute-start.11 = (bf16[2,256,128]{2,1,0:T(8,128)(2,1)S(1)}, bf16[2,256,128]{2,1,0:T(8,128)(2,1)S(1)}, u32[]{:S(2)}, u32[]{:S(2)}) collective-permute-start(bf16[2,256,128]{2,1,0:T(8,128)(2,1)S(1)} %get-tuple-element.68), channel_id=1, source_target_pairs={{0,2},{1,3},{2,0},{3,1},{4,6},{5,7},{6,4},{7,5},{8,10},{9,11},{10,... | collective-permute-start | bytes 393224 | tf_op jit(solution)/shard_map/ppermute | solution.py:574
  47.6 0.4 collective-permute-done.5.got_ref
  47.9 0.1 spread_sums.1
  48.0 1.1 %collective-permute-start.6 = (bf16[256,128]{1,0:T(8,128)(2,1)S(1)}, bf16[256,128]{1,0:T(8,128)(2,1)S(1)}, u32[]{:S(2)}, u32[]{:S(2)}) collective-permute-start(bf16[256,128]{1,0:T(8,128)(2,1)S(1)} %get-tuple-element.62), channel_id=1, source_target_pairs={{0,2},{1,3},{2,0},{3,1},{4,6},{5,7},{6,4},{7,5},{8,10},{9,11},{10,... | collective-permute-start | bytes 196616 | tf_op jit(solution)/shard_map/ppermute | solution.py:574
  49.0 0.5 collective-permute-start.7
  49.5 2.9 %collective-permute-start.8 = (bf16[256,128]{1,0:T(8,128)(2,1)S(1)}, bf16[256,128]{1,0:T(8,128)(2,1)S(1)}, u32[]{:S(2)}, u32[]{:S(2)}) collective-permute-start(bf16[256,128]{1,0:T(8,128)(2,1)S(1)} %get-tuple-element.64), channel_id=1, source_target_pairs={{0,6},{1,7},{2,4},{3,5},{4,2},{5,3},{6,0},{7,1},{8,14},{9,15},{10,... | collective-permute-start | bytes 196616 | tf_op jit(solution)/shard_map/ppermute | solution.py:574
  52.4 1.3 %collective-permute-done.11.got_ref = bf16[2,256,128]{2,1,0:T(8,128)(2,1)S(1)} collective-permute-done((bf16[2,256,128]{2,1,0:T(8,128)(2,1)S(1)}, bf16[2,256,128]{2,1,0:T(8,128)(2,1)S(1)}, u32[]{:S(2)}, u32[]{:S(2)}) %collective-permute-start.11) | collective-permute-done | bytes 131104 | tf_op jit(solution)/shard_map/ppermute | solution.py:574
  53.8 0.1 collective-permute-start.12
  53.8 0.7 %collective-permute-done.6.refs_1_ = bf16[256,128]{1,0:T(8,128)(2,1)S(1)} collective-permute-done((bf16[256,128]{1,0:T(8,128)(2,1)S(1)}, bf16[256,128]{1,0:T(8,128)(2,1)S(1)}, u32[]{:S(2)}, u32[]{:S(2)}) %collective-permute-start.6) | collective-permute-done | bytes 65568 | tf_op jit(solution)/shard_map/ppermute | solution.py:574
  54.6 4.4 %collective-permute-done.7.refs_2_ = bf16[256,128]{1,0:T(8,128)(2,1)S(1)} collective-permute-done((bf16[256,128]{1,0:T(8,128)(2,1)S(1)}, bf16[256,128]{1,0:T(8,128)(2,1)S(1)}, u32[]{:S(2)}, u32[]{:S(2)}) %collective-permute-start.7) | collective-permute-done | bytes 65568 | tf_op jit(solution)/shard_map/ppermute | solution.py:574
  59.0 0.0 collective-permute-done.8.refs_3_
  59.0 1.5 %collective-permute-start.9 = (bf16[272,128]{1,0:T(8,128)(2,1)S(1)}, bf16[272,128]{1,0:T(8,128)(2,1)S(1)}, u32[]{:S(2)}, u32[]{:S(2)}) collective-permute-start(bf16[272,128]{1,0:T(8,128)(2,1)S(1)} %line_sums_loss.1), channel_id=1, source_target_pairs={{0,1},{1,9},{2,3},{3,11},{4,5},{5,13},{6,7},{7,15},{8,0},{9,8},{10... | collective-permute-start | bytes 208904 | tf_op jit(solution)/shard_map/ppermute | solution.py:434
  60.5 0.2 collective-permute-done.12.refs_1_
  60.8 1.5 %collective-permute-start.13 = (bf16[256,128]{1,0:T(8,128)(2,1)S(1)}, bf16[256,128]{1,0:T(8,128)(2,1)S(1)}, u32[]{:S(2)}, u32[]{:S(2)}) collective-permute-start(bf16[256,128]{1,0:T(8,128)(2,1)S(1)} %line_sums.1), channel_id=1, source_target_pairs={{0,1},{1,9},{2,3},{3,11},{4,5},{5,13},{6,7},{7,15},{8,0},{9,8},{10... | collective-permute-start | bytes 196616 | tf_op jit(solution)/shard_map/ppermute | solution.py:434
  62.3 0.2 collective-permute-done.9.low_ref
  62.5 1.7 %collective-permute-done.13.high_ref = bf16[256,128]{1,0:T(8,128)(2,1)S(1)} collective-permute-done((bf16[256,128]{1,0:T(8,128)(2,1)S(1)}, bf16[256,128]{1,0:T(8,128)(2,1)S(1)}, u32[]{:S(2)}, u32[]{:S(2)}) %collective-permute-start.13) | collective-permute-done | bytes 65568 | tf_op jit(solution)/shard_map/ppermute | solution.py:434
  64.2 0.7 %home_again.1 = (f32[4,128]{1,0:T(4,128)}, bf16[512,128]{1,0:T(8,128)(2,1)}) custom-call(bf16[272,128]{1,0:T(8,128)(2,1)S(1)} %collective-permute-done.9.low_ref, bf16[256,128]{1,0:T(8,128)(2,1)S(1)} %collective-permute-done.13.high_ref), custom_call_target="tpu_custom_call" | custom-call | tf_op jit(solution)/shard_map/home_again/pallas_call | solution.py:402
  (8 shorter events, 0.1 us)
Async XLA Ops:
  0.6 21.6 %copy-start.3 = (s32[512,8]{0,1:T(8,128)S(1)}, s32[512,8]{0,1:T(8,128)}, u32[]{:S(2)}) copy-start(s32[512,8]{0,1:T(8,128)} %param.9) | copy-start | bytes 49156
  0.6 21.6 %copy-start = (bf16[4,256,1024]{2,1,0:T(8,128)(2,1)S(1)}, bf16[4,256,1024]{2,1,0:T(8,128)(2,1)}, u32[]{:S(2)}) copy-start(bf16[4,256,1024]{2,1,0:T(8,128)(2,1)} %weights_ref.5) | copy-start | bytes 6291460
  0.7 21.6 %copy-start.2 = (s32[16,16]{1,0:T(8,128)S(1)}, s32[16,16]{1,0:T(8,128)}, u32[]{:S(2)}) copy-start(s32[16,16]{1,0:T(8,128)} %lists_hbm.3) | copy-start | bytes 3076
  0.7 21.6 %copy-start.4 = (s32[128]{0:T(128)S(1)}, s32[128]{0:T(128)}, u32[]{:S(2)}) copy-start(s32[128]{0:T(128)} %slot_hbm.3) | copy-start | bytes 1540
  0.7 23.5 %collective-permute-start = (bf16[4,128,1024]{2,1,0:T(8,128)(2,1)}, bf16[4,128,1024]{2,1,0:T(8,128)(2,1)S(1)}, u32[]{:S(2)}, u32[]{:S(2)}) collective-permute-start(bf16[4,128,1024]{2,1,0:T(8,128)(2,1)} %bitcast.5), channel_id=1, source_target_pairs={{0,8},{8,0},{16,24},{24,16},{1,9},{9,1},{17,25},{25,17},{2,10},{10... | collective-permute-start | bytes 3145736 | tf_op jit(solution)/shard_map/ppermute | solution.py:439
  3.7 20.4 %copy-start.1 = (bf16[512,1024]{1,0:T(8,128)(2,1)S(1)}, bf16[512,1024]{1,0:T(8,128)(2,1)}, u32[]{:S(2)}) copy-start(bf16[512,1024]{1,0:T(8,128)(2,1)} %param.5) | copy-start | bytes 3145732
  3.8 16.6 %collective-permute-start.2 = (bf16[256,1024]{1,0:T(8,128)(2,1)}, bf16[256,1024]{1,0:T(8,128)(2,1)S(1)}, u32[]{:S(2)}, u32[]{:S(2)}) collective-permute-start(bf16[256,1024]{1,0:T(8,128)(2,1)} %pick_far.3), channel_id=1, source_target_pairs={{0,17},{1,16},{2,19},{3,18},{4,21},{5,20},{6,23},{7,22},{8,25},{9,... | collective-permute-start | bytes 1572872 | tf_op jit(solution)/shard_map/ppermute | solution.py:479
  9.9 18.6 %collective-permute-start.4 = (bf16[256,1024]{1,0:T(8,128)(2,1)}, bf16[256,1024]{1,0:T(8,128)(2,1)S(1)}, u32[]{:S(2)}, u32[]{:S(2)}) collective-permute-start(bf16[256,1024]{1,0:T(8,128)(2,1)} %get-tuple-element.47), channel_id=1, source_target_pairs={{0,16},{1,17},{2,18},{3,19},{4,20},{5,21},{6,22},{7,23},{8,9},{9,8... | collective-permute-start | bytes 1572872 | tf_op jit(solution)/shard_map/ppermute | solution.py:479
  20.3 11.2 %collective-permute-start.3 = (bf16[256,1024]{1,0:T(8,128)(2,1)}, bf16[256,1024]{1,0:T(8,128)(2,1)S(1)}, u32[]{:S(2)}, u32[]{:S(2)}) collective-permute-start(bf16[256,1024]{1,0:T(8,128)(2,1)} %get-tuple-element.46), channel_id=1, source_target_pairs={{0,1},{1,0},{2,3},{3,2},{4,5},{5,4},{6,7},{7,6},{8,24},{9,25},{10,... | collective-permute-start | bytes 1572872 | tf_op jit(solution)/shard_map/ppermute | solution.py:479
  22.3 1.9 %collective-permute-start.1 = (s32[4,8,128]{2,1,0:T(8,128)S(1)}, s32[4,8,128]{2,1,0:T(8,128)S(1)}, u32[]{:S(2)}, u32[]{:S(2)}) collective-permute-start(s32[4,8,128]{2,1,0:T(8,128)S(1)} %bitcast.7), channel_id=1, source_target_pairs={{0,8},{8,0},{16,24},{24,16},{1,9},{9,1},{17,25},{25,17},{2,10},{10... | collective-permute-start | bytes 49160 | tf_op jit(solution)/shard_map/ppermute | solution.py:440
  44.3 2.4 %collective-permute-start.10 = (bf16[4,256,128]{2,1,0:T(8,128)(2,1)S(1)}, bf16[4,256,128]{2,1,0:T(8,128)(2,1)S(1)}, u32[]{:S(2)}, u32[]{:S(2)}) collective-permute-start(bf16[4,256,128]{2,1,0:T(8,128)(2,1)S(1)} %get-tuple-element.66), channel_id=1, source_target_pairs={{0,8},{8,0},{16,24},{24,16},{1,9},{9,1},{17,25},{25,17},{2,10},{10... | collective-permute-start | bytes 786440 | tf_op jit(solution)/shard_map/ppermute | solution.py:571
  46.2 1.7 %collective-permute-start.5 = (bf16[4,256,128]{2,1,0:T(8,128)(2,1)S(1)}, bf16[4,256,128]{2,1,0:T(8,128)(2,1)S(1)}, u32[]{:S(2)}, u32[]{:S(2)}) collective-permute-start(bf16[4,256,128]{2,1,0:T(8,128)(2,1)S(1)} %get-tuple-element.60), channel_id=1, source_target_pairs={{0,8},{8,0},{16,24},{24,16},{1,9},{9,1},{17,25},{25,17},{2,10},{10... | collective-permute-start | bytes 786440 | tf_op jit(solution)/shard_map/ppermute | solution.py:571
  46.8 6.9 %collective-permute-start.11 = (bf16[2,256,128]{2,1,0:T(8,128)(2,1)S(1)}, bf16[2,256,128]{2,1,0:T(8,128)(2,1)S(1)}, u32[]{:S(2)}, u32[]{:S(2)}) collective-permute-start(bf16[2,256,128]{2,1,0:T(8,128)(2,1)S(1)} %get-tuple-element.68), channel_id=1, source_target_pairs={{0,2},{1,3},{2,0},{3,1},{4,6},{5,7},{6,4},{7,5},{8,10},{9,11},{10,... | collective-permute-start | bytes 393224 | tf_op jit(solution)/shard_map/ppermute | solution.py:574
  48.0 6.6 %collective-permute-start.6 = (bf16[256,128]{1,0:T(8,128)(2,1)S(1)}, bf16[256,128]{1,0:T(8,128)(2,1)S(1)}, u32[]{:S(2)}, u32[]{:S(2)}) collective-permute-start(bf16[256,128]{1,0:T(8,128)(2,1)S(1)} %get-tuple-element.62), channel_id=1, source_target_pairs={{0,2},{1,3},{2,0},{3,1},{4,6},{5,7},{6,4},{7,5},{8,10},{9,11},{10,... | collective-permute-start | bytes 196616 | tf_op jit(solution)/shard_map/ppermute | solution.py:574
  49.0 9.9 %collective-permute-start.7 = (bf16[256,128]{1,0:T(8,128)(2,1)S(1)}, bf16[256,128]{1,0:T(8,128)(2,1)S(1)}, u32[]{:S(2)}, u32[]{:S(2)}) collective-permute-start(bf16[256,128]{1,0:T(8,128)(2,1)S(1)} %get-tuple-element.63), channel_id=1, source_target_pairs={{0,4},{1,5},{2,6},{3,7},{4,0},{5,1},{6,2},{7,3},{8,12},{9,13},{10,... | collective-permute-start | bytes 196616 | tf_op jit(solution)/shard_map/ppermute | solution.py:574
  49.5 9.4 %collective-permute-start.8 = (bf16[256,128]{1,0:T(8,128)(2,1)S(1)}, bf16[256,128]{1,0:T(8,128)(2,1)S(1)}, u32[]{:S(2)}, u32[]{:S(2)}) collective-permute-start(bf16[256,128]{1,0:T(8,128)(2,1)S(1)} %get-tuple-element.64), channel_id=1, source_target_pairs={{0,6},{1,7},{2,4},{3,5},{4,2},{5,3},{6,0},{7,1},{8,14},{9,15},{10,... | collective-permute-start | bytes 196616 | tf_op jit(solution)/shard_map/ppermute | solution.py:574
  53.8 7.0 %collective-permute-start.12 = (bf16[256,128]{1,0:T(8,128)(2,1)S(1)}, bf16[256,128]{1,0:T(8,128)(2,1)S(1)}, u32[]{:S(2)}, u32[]{:S(2)}) collective-permute-start(bf16[256,128]{1,0:T(8,128)(2,1)S(1)} %get-tuple-element.71), channel_id=1, source_target_pairs={{0,4},{1,5},{2,6},{3,7},{4,0},{5,1},{6,2},{7,3},{8,12},{9,13},{10,... | collective-permute-start | bytes 196616 | tf_op jit(solution)/shard_map/ppermute | solution.py:574
  59.0 3.4 %collective-permute-start.9 = (bf16[272,128]{1,0:T(8,128)(2,1)S(1)}, bf16[272,128]{1,0:T(8,128)(2,1)S(1)}, u32[]{:S(2)}, u32[]{:S(2)}) collective-permute-start(bf16[272,128]{1,0:T(8,128)(2,1)S(1)} %line_sums_loss.1), channel_id=1, source_target_pairs={{0,1},{1,9},{2,3},{3,11},{4,5},{5,13},{6,7},{7,15},{8,0},{9,8},{10... | collective-permute-start | bytes 208904 | tf_op jit(solution)/shard_map/ppermute | solution.py:434
  60.8 3.4 %collective-permute-start.13 = (bf16[256,128]{1,0:T(8,128)(2,1)S(1)}, bf16[256,128]{1,0:T(8,128)(2,1)S(1)}, u32[]{:S(2)}, u32[]{:S(2)}) collective-permute-start(bf16[256,128]{1,0:T(8,128)(2,1)S(1)} %line_sums.1), channel_id=1, source_target_pairs={{0,1},{1,9},{2,3},{3,11},{4,5},{5,13},{6,7},{7,15},{8,0},{9,8},{10... | collective-permute-start | bytes 196616 | tf_op jit(solution)/shard_map/ppermute | solution.py:434

commit v2 on v1

--- a/solution.py
+++ b/solution.py
@@ -584,7 +584,7 @@
     spread = call(
         spread_kernel, "spread_sums", [wide] + [narrow] * (pairs - 1), [vmem()] * 2, halves[0]
     )
-    low = [spread[0]] + [hop(x, 2 * j + 2) for j, x in enumerate(spread[1:])]
+    low = [spread[0]] + [hop(spread[j], 2 * j) for j in range(pairs - 1, 0, -1)]
     got, *_ = lax.optimization_barrier((got, *spread))
     own, send = call(step_kernel, "step_sums", [wide, narrow], [vmem()] * 2, (keep, got))
     high = [own, hop(send, 4)]

time: 65 us -> 64 us (0.985)
  waiting for transfers between devices: 20.6 us -> 19.9 us
    ppermute x5, waiting for transfers between devices: 6.64 us -> 5.93 us  [hop(): return lax.ppermute(x, 'label', [(i, i ^ mask) for i in range(lab_count)])]
  transfers between devices with their start and end apart: 14 -> 14, of which waited for: 9 -> 7; matrix products, arithmetic and copies ran while one was open for 0% -> 0% of each run, Pallas kernels for 22% -> 23%
where the time goes in v2:
time: 64 us; the launch traced here: 63.8 us
  waiting for transfers between devices  19.9 us (31%)
  Pallas kernels  17.4 us (27%)
  starting transfers between devices  15.2 us (24%)
  blocking collectives  10.5 us (16%)
  between operations  0.8 us (1%)
    pallas_call x17, Pallas kernels, call(): pl.pallas_call(kernel, out_shape=out_shape, in_specs=in_specs, out_specs=...  17.4 us
    ppermute x3, waiting for transfers between devices, shards(): rows.append(lax.ppermute(x, both, plan.pairs(k)))  11.7 us
    all_to_all x1, blocking collectives, shards(): lax.all_to_all(stats[0], both, split_axis=0, concat_axis=0, axis_index_gr...  10.5 us
    ppermute x3, starting transfers between devices, shards(): rows.append(lax.ppermute(x, both, plan.pairs(k)))  6.05 us
    ppermute x5, waiting for transfers between devices, hop(): return lax.ppermute(x, 'label', [(i, i ^ mask) for i in range(lab_count)])  5.93 us
    ppermute x5, starting transfers between devices, hop(): return lax.ppermute(x, 'label', [(i, i ^ mask) for i in range(lab_count)])  5.61 us
    ppermute x2, starting transfers between devices, move(): return lax.ppermute(x, both, pairs)  2.42 us
    ppermute x2, waiting for transfers between devices, move(): return lax.ppermute(x, both, pairs)  1.91 us
  transfers between devices with their start and end apart: 14, of which 7 were waited for; matrix products, arithmetic and copies ran while one was open for 0% of the time, Pallas kernels for 23%

profile of v2, /device:TPU:0, one launch (start us, length us, event | category | flops | bytes accessed | tf_op | source)
XLA Modules:
  0.0 63.8 jit_solution(10171220609906513177)
XLA Ops:
  0.6 0.0 copy-start
  0.7 0.0 copy-start.2
  0.7 0.0 copy-start.4
  0.7 0.5 collective-permute-start
  1.2 2.5 %pick_far.3 = bf16[256,1024]{1,0:T(8,128)(2,1)} custom-call(s32[16,16]{1,0:T(8,128)} %lists_hbm.3, s32[128]{0:T(128)} %slot_hbm.3, bf16[4,256,1024]{2,1,0:T(8,128)(2,1)} %weights_ref.5), custom_call_target="tpu_custom_call" | custom-call | tf_op jit(solution)/shard_map/pick_far/pallas_call | solution.py:402
  3.7 0.0 copy-start.1
  3.8 3.6 %collective-permute-start.2 = (bf16[256,1024]{1,0:T(8,128)(2,1)}, bf16[256,1024]{1,0:T(8,128)(2,1)S(1)}, u32[]{:S(2)}, u32[]{:S(2)}) collective-permute-start(bf16[256,1024]{1,0:T(8,128)(2,1)} %pick_far.3), channel_id=1, source_target_pairs={{0,17},{1,16},{2,19},{3,18},{4,21},{5,20},{6,23},{7,22},{8,25},{9,... | collective-permute-start | bytes 1572872 | tf_op jit(solution)/shard_map/ppermute | solution.py:479
  7.3 2.6 %pick_far.2 = (bf16[256,1024]{1,0:T(8,128)(2,1)}, bf16[256,1024]{1,0:T(8,128)(2,1)}) custom-call(s32[16,16]{1,0:T(8,128)} %lists_hbm.3, s32[128]{0:T(128)} %slot_hbm.3, bf16[4,256,1024]{2,1,0:T(8,128)(2,1)} %weights_ref.5), custom_call_target="tpu_custom_call" | custom-call | tf_op jit(solution)/shard_map/pick_far/pallas_call | solution.py:402
  9.9 0.6 collective-permute-start.4
  10.5 9.8 %collective-permute-done.2.rest_0_.rest_5_ = bf16[256,1024]{1,0:T(8,128)(2,1)S(1)} collective-permute-done((bf16[256,1024]{1,0:T(8,128)(2,1)}, bf16[256,1024]{1,0:T(8,128)(2,1)S(1)}, u32[]{:S(2)}, u32[]{:S(2)}) %collective-permute-start.2) | collective-permute-done | bytes 524320 | tf_op jit(solution)/shard_map/ppermute | solution.py:479
  20.3 1.9 %collective-permute-start.3 = (bf16[256,1024]{1,0:T(8,128)(2,1)}, bf16[256,1024]{1,0:T(8,128)(2,1)S(1)}, u32[]{:S(2)}, u32[]{:S(2)}) collective-permute-start(bf16[256,1024]{1,0:T(8,128)(2,1)} %get-tuple-element.46), channel_id=1, source_target_pairs={{0,1},{1,0},{2,3},{3,2},{4,5},{5,4},{6,7},{7,6},{8,24},{9,25},{10,... | collective-permute-start | bytes 1572872 | tf_op jit(solution)/shard_map/ppermute | solution.py:479
  22.3 0.0 copy-done.3
  22.3 0.0 collective-permute-start.1
  22.3 1.9 %pick_near.1 = (s32[4,4]{1,0:T(4,128)S(1)}, bf16[256,1024]{1,0:T(8,128)(2,1)S(1)}) custom-call(s32[16,16]{1,0:T(8,128)S(1)} %copy-done.2, s32[128]{0:T(128)S(1)} %copy-done.4, bf16[4,256,1024]{2,1,0:T(8,128)(2,1)S(1)} %copy-done), custom_call_target="tpu_custom_call" | custom-call | tf_op jit(solution)/shard_map/pick_near/pallas_call | solution.py:402
  24.2 0.0 collective-permute-done.1.other_pos_ref
  24.2 0.0 collective-permute-done.other_feats_ref
  24.2 0.0 copy-done.1
  24.2 0.1 home.1
  24.3 1.9 %targets.1 = (f32[4,256,256]{2,1,0:T(8,128)S(1)}, f32[3,256,256]{2,1,0:T(8,128)S(1)}, bf16[1,1024,256]{2,1,0:T(8,128)(2,1)S(1)}) custom-call(s32[4,4]{1,0:T(4,128)S(1)} %get-tuple-element.39.table_ref, s32[4,8,128]{2,1,0:T(8,128)S(1)} %get-tuple-element.40.pos_ref, bf16[4,128,1024]{2,1,0:T(8,128)(2,1)S(1)} %get-tuple-element.41.feats_ref), custom_call_target="tpu_custom_call" | custom-call | tf_op jit(solution)/shard_map/targets/pallas_call | solution.py:402
  26.3 1.1 %logits.4 = (f32[1,256,256]{2,1,0:T(8,128)S(1)}, f32[1,3,4,128]{3,2,1,0:T(4,128)S(1)}) custom-call(s32[4,4]{1,0:T(4,128)S(1)} %get-tuple-element.39.table_ref, bf16[4,128,1024]{2,1,0:T(8,128)(2,1)S(1)} %get-tuple-element.41.feats_ref, f32[4,256,256]{2,1,0:T(8,128)S(1)} %get-tuple-element.42.hits_ref, bf16[256,1024]{1,0:T(8,128)(2,1)S(1)} %get-tuple-element.49.rest_0_.rest_4_), custom_call_target="tpu_custom_call" | custom-call | tf_op jit(solution)/shard_map/logits/pallas_call | solution.py:402
  27.4 1.1 %logits.5 = (f32[1,256,256]{2,1,0:T(8,128)S(1)}, f32[1,3,4,128]{3,2,1,0:T(4,128)S(1)}) custom-call(s32[4,4]{1,0:T(4,128)S(1)} %get-tuple-element.39.table_ref, bf16[4,128,1024]{2,1,0:T(8,128)(2,1)S(1)} %get-tuple-element.41.feats_ref, f32[4,256,256]{2,1,0:T(8,128)S(1)} %get-tuple-element.42.hits_ref, ...), custom_call_target="tpu_custom_call" | custom-call | tf_op jit(solution)/shard_map/logits/pallas_call | solution.py:402
  28.5 0.0 collective-permute-done.4.rest_0_.rest_6_
  28.5 1.1 %logits.6 = (f32[1,256,256]{2,1,0:T(8,128)S(1)}, f32[1,3,4,128]{3,2,1,0:T(4,128)S(1)}) custom-call(s32[4,4]{1,0:T(4,128)S(1)} %get-tuple-element.39.table_ref, bf16[4,128,1024]{2,1,0:T(8,128)(2,1)S(1)} %get-tuple-element.41.feats_ref, f32[4,256,256]{2,1,0:T(8,128)S(1)} %get-tuple-element.42.hits_ref, ...), custom_call_target="tpu_custom_call" | custom-call | tf_op jit(solution)/shard_map/logits/pallas_call | solution.py:402
  29.6 1.9 %collective-permute-done.3.rest_0_.rest_7_ = bf16[256,1024]{1,0:T(8,128)(2,1)S(1)} collective-permute-done((bf16[256,1024]{1,0:T(8,128)(2,1)}, bf16[256,1024]{1,0:T(8,128)(2,1)S(1)}, u32[]{:S(2)}, u32[]{:S(2)}) %collective-permute-start.3) | collective-permute-done | bytes 524320 | tf_op jit(solution)/shard_map/ppermute | solution.py:479
  31.5 1.0 %logits.7 = (f32[1,256,256]{2,1,0:T(8,128)S(1)}, f32[8,3,4,128]{3,2,1,0:T(4,128)S(1)}) custom-call(s32[4,4]{1,0:T(4,128)S(1)} %get-tuple-element.39.table_ref, bf16[1,1024,256]{2,1,0:T(8,128)(2,1)S(1)} %get-tuple-element.44.feats_ref, f32[4,256,256]{2,1,0:T(8,128)S(1)} %get-tuple-element.42.hits_ref, ...), custom_call_target="tpu_custom_call" | custom-call | tf_op jit(solution)/shard_map/logits/pallas_call | solution.py:402
  32.4 10.5 %all_to_all.5.stats_ref = f32[8,3,4,128]{3,2,1,0:T(4,128)S(1)} all-to-all(f32[8,3,4,128]{3,2,1,0:T(4,128)S(1)} %get-tuple-element.53), channel_id=1, replica_groups={{0,8,2,10,4,12,6,14},{1,9,3,11,5,13,7,15},{16,24,18,26,20,28,22,30},{17..., dimensions={0} | all-to-all | bytes 98304 | tf_op jit(solution)/shard_map/all_to_all | solution.py:545
  43.0 1.4 %grads.2 = (f32[4,128]{1,0:T(4,128)S(1)}, f32[4,256,128]{2,1,0:T(8,128)S(1)}, bf16[4,256,128]{2,1,0:T(8,128)(2,1)S(1)}) custom-call(s32[4,4]{1,0:T(4,128)S(1)} %get-tuple-element.39.table_ref, f32[4,256,256]{2,1,0:T(8,128)S(1)} %get-tuple-element.42.hits_ref, f32[3,256,256]{2,1,0:T(8,128)S(1)} %get-tuple-element.43.shares_ref, ...), custom_call_target="tpu_custom_call" | custom-call | tf_op jit(solution)/shard_map/grads/pallas_call | solution.py:402
  44.3 0.1 collective-permute-start.10
  44.4 1.8 %grads.3 = (f32[4,128]{1,0:T(4,128)}, f32[4,256,128]{2,1,0:T(8,128)S(1)}, bf16[4,256,128]{2,1,0:T(8,128)(2,1)S(1)}) custom-call(s32[4,4]{1,0:T(4,128)S(1)} %get-tuple-element.39.table_ref, f32[4,256,256]{2,1,0:T(8,128)S(1)} %get-tuple-element.42.hits_ref, f32[3,256,256]{2,1,0:T(8,128)S(1)} %get-tuple-element.43.shares_ref, ...), custom_call_target="tpu_custom_call" | custom-call | tf_op jit(solution)/shard_map/grads/pallas_call | solution.py:402
  46.2 0.5 collective-permute-start.5
  46.7 0.0 collective-permute-done.10.got_ref
  46.8 0.8 %collective-permute-start.11 = (bf16[2,256,128]{2,1,0:T(8,128)(2,1)S(1)}, bf16[2,256,128]{2,1,0:T(8,128)(2,1)S(1)}, u32[]{:S(2)}, u32[]{:S(2)}) collective-permute-start(bf16[2,256,128]{2,1,0:T(8,128)(2,1)S(1)} %get-tuple-element.68), channel_id=1, source_target_pairs={{0,2},{1,3},{2,0},{3,1},{4,6},{5,7},{6,4},{7,5},{8,10},{9,11},{10,... | collective-permute-start | bytes 393224 | tf_op jit(solution)/shard_map/ppermute | solution.py:574
  47.6 0.4 collective-permute-done.5.got_ref
  47.9 0.1 spread_sums.1
  48.0 1.0 %collective-permute-start.6 = (bf16[256,128]{1,0:T(8,128)(2,1)S(1)}, bf16[256,128]{1,0:T(8,128)(2,1)S(1)}, u32[]{:S(2)}, u32[]{:S(2)}) collective-permute-start(bf16[256,128]{1,0:T(8,128)(2,1)S(1)} %get-tuple-element.62), channel_id=1, source_target_pairs={{0,6},{1,7},{2,4},{3,5},{4,2},{5,3},{6,0},{7,1},{8,14},{9,15},{10,... | collective-permute-start | bytes 196616 | tf_op jit(solution)/shard_map/ppermute | solution.py:574
  48.9 1.5 %collective-permute-start.7 = (bf16[256,128]{1,0:T(8,128)(2,1)S(1)}, bf16[256,128]{1,0:T(8,128)(2,1)S(1)}, u32[]{:S(2)}, u32[]{:S(2)}) collective-permute-start(bf16[256,128]{1,0:T(8,128)(2,1)S(1)} %get-tuple-element.63), channel_id=1, source_target_pairs={{0,4},{1,5},{2,6},{3,7},{4,0},{5,1},{6,2},{7,3},{8,12},{9,13},{10,... | collective-permute-start | bytes 196616 | tf_op jit(solution)/shard_map/ppermute | solution.py:574
  50.5 2.0 %collective-permute-start.8 = (bf16[256,128]{1,0:T(8,128)(2,1)S(1)}, bf16[256,128]{1,0:T(8,128)(2,1)S(1)}, u32[]{:S(2)}, u32[]{:S(2)}) collective-permute-start(bf16[256,128]{1,0:T(8,128)(2,1)S(1)} %get-tuple-element.64), channel_id=1, source_target_pairs={{0,2},{1,3},{2,0},{3,1},{4,6},{5,7},{6,4},{7,5},{8,10},{9,11},{10,... | collective-permute-start | bytes 196616 | tf_op jit(solution)/shard_map/ppermute | solution.py:574
  52.4 0.0 collective-permute-done.11.got_ref
  52.5 0.4 collective-permute-start.12
  52.9 2.0 %collective-permute-done.6.refs_1_ = bf16[256,128]{1,0:T(8,128)(2,1)S(1)} collective-permute-done((bf16[256,128]{1,0:T(8,128)(2,1)S(1)}, bf16[256,128]{1,0:T(8,128)(2,1)S(1)}, u32[]{:S(2)}, u32[]{:S(2)}) %collective-permute-start.6) | collective-permute-done | bytes 65568 | tf_op jit(solution)/shard_map/ppermute | solution.py:574
  54.9 3.9 %collective-permute-done.7.refs_2_ = bf16[256,128]{1,0:T(8,128)(2,1)S(1)} collective-permute-done((bf16[256,128]{1,0:T(8,128)(2,1)S(1)}, bf16[256,128]{1,0:T(8,128)(2,1)S(1)}, u32[]{:S(2)}, u32[]{:S(2)}) %collective-permute-start.7) | collective-permute-done | bytes 65568 | tf_op jit(solution)/shard_map/ppermute | solution.py:574
  58.8 0.0 collective-permute-done.8.refs_3_
  58.8 1.5 %collective-permute-start.9 = (bf16[272,128]{1,0:T(8,128)(2,1)S(1)}, bf16[272,128]{1,0:T(8,128)(2,1)S(1)}, u32[]{:S(2)}, u32[]{:S(2)}) collective-permute-start(bf16[272,128]{1,0:T(8,128)(2,1)S(1)} %line_sums_loss.1), channel_id=1, source_target_pairs={{0,1},{1,9},{2,3},{3,11},{4,5},{5,13},{6,7},{7,15},{8,0},{9,8},{10... | collective-permute-start | bytes 208904 | tf_op jit(solution)/shard_map/ppermute | solution.py:434
  60.3 0.0 collective-permute-done.12.refs_1_
  60.4 0.9 %collective-permute-start.13 = (bf16[256,128]{1,0:T(8,128)(2,1)S(1)}, bf16[256,128]{1,0:T(8,128)(2,1)S(1)}, u32[]{:S(2)}, u32[]{:S(2)}) collective-permute-start(bf16[256,128]{1,0:T(8,128)(2,1)S(1)} %line_sums.1), channel_id=1, source_target_pairs={{0,1},{1,9},{2,3},{3,11},{4,5},{5,13},{6,7},{7,15},{8,0},{9,8},{10... | collective-permute-start | bytes 196616 | tf_op jit(solution)/shard_map/ppermute | solution.py:434
  61.3 1.0 %collective-permute-done.9.low_ref = bf16[272,128]{1,0:T(8,128)(2,1)S(1)} collective-permute-done((bf16[272,128]{1,0:T(8,128)(2,1)S(1)}, bf16[272,128]{1,0:T(8,128)(2,1)S(1)}, u32[]{:S(2)}, u32[]{:S(2)}) %collective-permute-start.9) | collective-permute-done | bytes 69664 | tf_op jit(solution)/shard_map/ppermute | solution.py:434
  62.3 0.9 %collective-permute-done.13.high_ref = bf16[256,128]{1,0:T(8,128)(2,1)S(1)} collective-permute-done((bf16[256,128]{1,0:T(8,128)(2,1)S(1)}, bf16[256,128]{1,0:T(8,128)(2,1)S(1)}, u32[]{:S(2)}, u32[]{:S(2)}) %collective-permute-start.13) | collective-permute-done | bytes 65568 | tf_op jit(solution)/shard_map/ppermute | solution.py:434
  63.2 0.7 %home_again.1 = (f32[4,128]{1,0:T(4,128)}, bf16[512,128]{1,0:T(8,128)(2,1)}) custom-call(bf16[272,128]{1,0:T(8,128)(2,1)S(1)} %collective-permute-done.9.low_ref, bf16[256,128]{1,0:T(8,128)(2,1)S(1)} %collective-permute-done.13.high_ref), custom_call_target="tpu_custom_call" | custom-call | tf_op jit(solution)/shard_map/home_again/pallas_call | solution.py:402
  (8 shorter events, 0.1 us)
Async XLA Ops:
  0.6 21.6 %copy-start.3 = (s32[512,8]{0,1:T(8,128)S(1)}, s32[512,8]{0,1:T(8,128)}, u32[]{:S(2)}) copy-start(s32[512,8]{0,1:T(8,128)} %param.9) | copy-start | bytes 49156
  0.6 21.6 %copy-start = (bf16[4,256,1024]{2,1,0:T(8,128)(2,1)S(1)}, bf16[4,256,1024]{2,1,0:T(8,128)(2,1)}, u32[]{:S(2)}) copy-start(bf16[4,256,1024]{2,1,0:T(8,128)(2,1)} %weights_ref.5) | copy-start | bytes 6291460
  0.7 21.6 %copy-start.2 = (s32[16,16]{1,0:T(8,128)S(1)}, s32[16,16]{1,0:T(8,128)}, u32[]{:S(2)}) copy-start(s32[16,16]{1,0:T(8,128)} %lists_hbm.3) | copy-start | bytes 3076
  0.7 21.6 %copy-start.4 = (s32[128]{0:T(128)S(1)}, s32[128]{0:T(128)}, u32[]{:S(2)}) copy-start(s32[128]{0:T(128)} %slot_hbm.3) | copy-start | bytes 1540
  0.7 23.5 %collective-permute-start = (bf16[4,128,1024]{2,1,0:T(8,128)(2,1)}, bf16[4,128,1024]{2,1,0:T(8,128)(2,1)S(1)}, u32[]{:S(2)}, u32[]{:S(2)}) collective-permute-start(bf16[4,128,1024]{2,1,0:T(8,128)(2,1)} %bitcast.5), channel_id=1, source_target_pairs={{0,8},{8,0},{16,24},{24,16},{1,9},{9,1},{17,25},{25,17},{2,10},{10... | collective-permute-start | bytes 3145736 | tf_op jit(solution)/shard_map/ppermute | solution.py:439
  3.7 20.4 %copy-start.1 = (bf16[512,1024]{1,0:T(8,128)(2,1)S(1)}, bf16[512,1024]{1,0:T(8,128)(2,1)}, u32[]{:S(2)}) copy-start(bf16[512,1024]{1,0:T(8,128)(2,1)} %param.5) | copy-start | bytes 3145732
  3.8 16.6 %collective-permute-start.2 = (bf16[256,1024]{1,0:T(8,128)(2,1)}, bf16[256,1024]{1,0:T(8,128)(2,1)S(1)}, u32[]{:S(2)}, u32[]{:S(2)}) collective-permute-start(bf16[256,1024]{1,0:T(8,128)(2,1)} %pick_far.3), channel_id=1, source_target_pairs={{0,17},{1,16},{2,19},{3,18},{4,21},{5,20},{6,23},{7,22},{8,25},{9,... | collective-permute-start | bytes 1572872 | tf_op jit(solution)/shard_map/ppermute | solution.py:479
  9.9 18.6 %collective-permute-start.4 = (bf16[256,1024]{1,0:T(8,128)(2,1)}, bf16[256,1024]{1,0:T(8,128)(2,1)S(1)}, u32[]{:S(2)}, u32[]{:S(2)}) collective-permute-start(bf16[256,1024]{1,0:T(8,128)(2,1)} %get-tuple-element.47), channel_id=1, source_target_pairs={{0,16},{1,17},{2,18},{3,19},{4,20},{5,21},{6,22},{7,23},{8,9},{9,8... | collective-permute-start | bytes 1572872 | tf_op jit(solution)/shard_map/ppermute | solution.py:479
  20.3 11.2 %collective-permute-start.3 = (bf16[256,1024]{1,0:T(8,128)(2,1)}, bf16[256,1024]{1,0:T(8,128)(2,1)S(1)}, u32[]{:S(2)}, u32[]{:S(2)}) collective-permute-start(bf16[256,1024]{1,0:T(8,128)(2,1)} %get-tuple-element.46), channel_id=1, source_target_pairs={{0,1},{1,0},{2,3},{3,2},{4,5},{5,4},{6,7},{7,6},{8,24},{9,25},{10,... | collective-permute-start | bytes 1572872 | tf_op jit(solution)/shard_map/ppermute | solution.py:479
  22.3 1.9 %collective-permute-start.1 = (s32[4,8,128]{2,1,0:T(8,128)S(1)}, s32[4,8,128]{2,1,0:T(8,128)S(1)}, u32[]{:S(2)}, u32[]{:S(2)}) collective-permute-start(s32[4,8,128]{2,1,0:T(8,128)S(1)} %bitcast.7), channel_id=1, source_target_pairs={{0,8},{8,0},{16,24},{24,16},{1,9},{9,1},{17,25},{25,17},{2,10},{10... | collective-permute-start | bytes 49160 | tf_op jit(solution)/shard_map/ppermute | solution.py:440
  44.3 2.4 %collective-permute-start.10 = (bf16[4,256,128]{2,1,0:T(8,128)(2,1)S(1)}, bf16[4,256,128]{2,1,0:T(8,128)(2,1)S(1)}, u32[]{:S(2)}, u32[]{:S(2)}) collective-permute-start(bf16[4,256,128]{2,1,0:T(8,128)(2,1)S(1)} %get-tuple-element.66), channel_id=1, source_target_pairs={{0,8},{8,0},{16,24},{24,16},{1,9},{9,1},{17,25},{25,17},{2,10},{10... | collective-permute-start | bytes 786440 | tf_op jit(solution)/shard_map/ppermute | solution.py:571
  46.2 1.7 %collective-permute-start.5 = (bf16[4,256,128]{2,1,0:T(8,128)(2,1)S(1)}, bf16[4,256,128]{2,1,0:T(8,128)(2,1)S(1)}, u32[]{:S(2)}, u32[]{:S(2)}) collective-permute-start(bf16[4,256,128]{2,1,0:T(8,128)(2,1)S(1)} %get-tuple-element.60), channel_id=1, source_target_pairs={{0,8},{8,0},{16,24},{24,16},{1,9},{9,1},{17,25},{25,17},{2,10},{10... | collective-permute-start | bytes 786440 | tf_op jit(solution)/shard_map/ppermute | solution.py:571
  46.8 5.7 %collective-permute-start.11 = (bf16[2,256,128]{2,1,0:T(8,128)(2,1)S(1)}, bf16[2,256,128]{2,1,0:T(8,128)(2,1)S(1)}, u32[]{:S(2)}, u32[]{:S(2)}) collective-permute-start(bf16[2,256,128]{2,1,0:T(8,128)(2,1)S(1)} %get-tuple-element.68), channel_id=1, source_target_pairs={{0,2},{1,3},{2,0},{3,1},{4,6},{5,7},{6,4},{7,5},{8,10},{9,11},{10,... | collective-permute-start | bytes 393224 | tf_op jit(solution)/shard_map/ppermute | solution.py:574
  48.0 6.9 %collective-permute-start.6 = (bf16[256,128]{1,0:T(8,128)(2,1)S(1)}, bf16[256,128]{1,0:T(8,128)(2,1)S(1)}, u32[]{:S(2)}, u32[]{:S(2)}) collective-permute-start(bf16[256,128]{1,0:T(8,128)(2,1)S(1)} %get-tuple-element.62), channel_id=1, source_target_pairs={{0,6},{1,7},{2,4},{3,5},{4,2},{5,3},{6,0},{7,1},{8,14},{9,15},{10,... | collective-permute-start | bytes 196616 | tf_op jit(solution)/shard_map/ppermute | solution.py:574
  48.9 9.8 %collective-permute-start.7 = (bf16[256,128]{1,0:T(8,128)(2,1)S(1)}, bf16[256,128]{1,0:T(8,128)(2,1)S(1)}, u32[]{:S(2)}, u32[]{:S(2)}) collective-permute-start(bf16[256,128]{1,0:T(8,128)(2,1)S(1)} %get-tuple-element.63), channel_id=1, source_target_pairs={{0,4},{1,5},{2,6},{3,7},{4,0},{5,1},{6,2},{7,3},{8,12},{9,13},{10,... | collective-permute-start | bytes 196616 | tf_op jit(solution)/shard_map/ppermute | solution.py:574
  50.5 8.3 %collective-permute-start.8 = (bf16[256,128]{1,0:T(8,128)(2,1)S(1)}, bf16[256,128]{1,0:T(8,128)(2,1)S(1)}, u32[]{:S(2)}, u32[]{:S(2)}) collective-permute-start(bf16[256,128]{1,0:T(8,128)(2,1)S(1)} %get-tuple-element.64), channel_id=1, source_target_pairs={{0,2},{1,3},{2,0},{3,1},{4,6},{5,7},{6,4},{7,5},{8,10},{9,11},{10,... | collective-permute-start | bytes 196616 | tf_op jit(solution)/shard_map/ppermute | solution.py:574
  52.5 7.9 %collective-permute-start.12 = (bf16[256,128]{1,0:T(8,128)(2,1)S(1)}, bf16[256,128]{1,0:T(8,128)(2,1)S(1)}, u32[]{:S(2)}, u32[]{:S(2)}) collective-permute-start(bf16[256,128]{1,0:T(8,128)(2,1)S(1)} %get-tuple-element.71), channel_id=1, source_target_pairs={{0,4},{1,5},{2,6},{3,7},{4,0},{5,1},{6,2},{7,3},{8,12},{9,13},{10,... | collective-permute-start | bytes 196616 | tf_op jit(solution)/shard_map/ppermute | solution.py:574
  58.8 3.5 %collective-permute-start.9 = (bf16[272,128]{1,0:T(8,128)(2,1)S(1)}, bf16[272,128]{1,0:T(8,128)(2,1)S(1)}, u32[]{:S(2)}, u32[]{:S(2)}) collective-permute-start(bf16[272,128]{1,0:T(8,128)(2,1)S(1)} %line_sums_loss.1), channel_id=1, source_target_pairs={{0,1},{1,9},{2,3},{3,11},{4,5},{5,13},{6,7},{7,15},{8,0},{9,8},{10... | collective-permute-start | bytes 208904 | tf_op jit(solution)/shard_map/ppermute | solution.py:434
  60.4 2.8 %collective-permute-start.13 = (bf16[256,128]{1,0:T(8,128)(2,1)S(1)}, bf16[256,128]{1,0:T(8,128)(2,1)S(1)}, u32[]{:S(2)}, u32[]{:S(2)}) collective-permute-start(bf16[256,128]{1,0:T(8,128)(2,1)S(1)} %line_sums.1), channel_id=1, source_target_pairs={{0,1},{1,9},{2,3},{3,11},{4,5},{5,13},{6,7},{7,15},{8,0},{9,8},{10... | collective-permute-start | bytes 196616 | tf_op jit(solution)/shard_map/ppermute | solution.py:434

commit v3 on v2

--- a/solution.py
+++ b/solution.py
@@ -584,7 +584,7 @@
     spread = call(
         spread_kernel, "spread_sums", [wide] + [narrow] * (pairs - 1), [vmem()] * 2, halves[0]
     )
-    low = [spread[0]] + [hop(spread[j], 2 * j) for j in range(pairs - 1, 0, -1)]
+    low = [spread[0]] + [hop(spread[j], 2 * j) for j in (2, 3, 1)]
     got, *_ = lax.optimization_barrier((got, *spread))
     own, send = call(step_kernel, "step_sums", [wide, narrow], [vmem()] * 2, (keep, got))
     high = [own, hop(send, 4)]

time: 64 us -> 64.7 us (1.011)
  waiting for transfers between devices: 19.9 us -> 20.9 us
    ppermute x5, waiting for transfers between devices: 5.93 us -> 6.93 us  [hop(): return lax.ppermute(x, 'label', [(i, i ^ mask) for i in range(lab_count)])]
    ppermute x5, starting transfers between devices: 5.61 us -> 4.66 us  [hop(): return lax.ppermute(x, 'label', [(i, i ^ mask) for i in range(lab_count)])]
  transfers between devices with their start and end apart: 14 -> 14, of which waited for: 7 -> 7; matrix products, arithmetic and copies ran while one was open for 0% -> 0% of each run, Pallas kernels for 23% -> 22%
where the time goes in v3:
time: 64.7 us; the launch traced here: 64.5 us
  waiting for transfers between devices  20.9 us (32%)
  Pallas kernels  17.4 us (27%)
  starting transfers between devices  14.8 us (23%)
  blocking collectives  10.5 us (16%)
  between operations  0.8 us (1%)
    pallas_call x17, Pallas kernels, call(): pl.pallas_call(kernel, out_shape=out_shape, in_specs=in_specs, out_specs=...  17.4 us
    ppermute x3, waiting for transfers between devices, shards(): rows.append(lax.ppermute(x, both, plan.pairs(k)))  11.7 us
    all_to_all x1, blocking collectives, shards(): lax.all_to_all(stats[0], both, split_axis=0, concat_axis=0, axis_index_gr...  10.5 us
    ppermute x5, waiting for transfers between devices, hop(): return lax.ppermute(x, 'label', [(i, i ^ mask) for i in range(lab_count)])  6.93 us
    ppermute x3, starting transfers between devices, shards(): rows.append(lax.ppermute(x, both, plan.pairs(k)))  6.05 us
    ppermute x5, starting transfers between devices, hop(): return lax.ppermute(x, 'label', [(i, i ^ mask) for i in range(lab_count)])  4.66 us
    ppermute x2, starting transfers between devices, move(): return lax.ppermute(x, both, pairs)  2.99 us
    ppermute x2, waiting for transfers between devices, move(): return lax.ppermute(x, both, pairs)  1.91 us
  transfers between devices with their start and end apart: 14, of which 7 were waited for; matrix products, arithmetic and copies ran while one was open for 0% of the time, Pallas kernels for 22%

profile of v3, /device:TPU:0, one launch (start us, length us, event | category | flops | bytes accessed | tf_op | source)
XLA Modules:
  0.0 64.5 jit_solution(1700084943729456885)
XLA Ops:
  0.6 0.0 copy-start
  0.7 0.0 copy-start.2
  0.7 0.0 copy-start.4
  0.7 0.5 collective-permute-start
  1.2 2.5 %pick_far.3 = bf16[256,1024]{1,0:T(8,128)(2,1)} custom-call(s32[16,16]{1,0:T(8,128)} %lists_hbm.3, s32[128]{0:T(128)} %slot_hbm.3, bf16[4,256,1024]{2,1,0:T(8,128)(2,1)} %weights_ref.5), custom_call_target="tpu_custom_call" | custom-call | tf_op jit(solution)/shard_map/pick_far/pallas_call | solution.py:402
  3.7 0.0 copy-start.1
  3.8 3.6 %collective-permute-start.2 = (bf16[256,1024]{1,0:T(8,128)(2,1)}, bf16[256,1024]{1,0:T(8,128)(2,1)S(1)}, u32[]{:S(2)}, u32[]{:S(2)}) collective-permute-start(bf16[256,1024]{1,0:T(8,128)(2,1)} %pick_far.3), channel_id=1, source_target_pairs={{0,17},{1,16},{2,19},{3,18},{4,21},{5,20},{6,23},{7,22},{8,25},{9,... | collective-permute-start | bytes 1572872 | tf_op jit(solution)/shard_map/ppermute | solution.py:479
  7.3 2.6 %pick_far.2 = (bf16[256,1024]{1,0:T(8,128)(2,1)}, bf16[256,1024]{1,0:T(8,128)(2,1)}) custom-call(s32[16,16]{1,0:T(8,128)} %lists_hbm.3, s32[128]{0:T(128)} %slot_hbm.3, bf16[4,256,1024]{2,1,0:T(8,128)(2,1)} %weights_ref.5), custom_call_target="tpu_custom_call" | custom-call | tf_op jit(solution)/shard_map/pick_far/pallas_call | solution.py:402
  9.9 0.6 collective-permute-start.4
  10.5 9.8 %collective-permute-done.2.rest_0_.rest_5_ = bf16[256,1024]{1,0:T(8,128)(2,1)S(1)} collective-permute-done((bf16[256,1024]{1,0:T(8,128)(2,1)}, bf16[256,1024]{1,0:T(8,128)(2,1)S(1)}, u32[]{:S(2)}, u32[]{:S(2)}) %collective-permute-start.2) | collective-permute-done | bytes 524320 | tf_op jit(solution)/shard_map/ppermute | solution.py:479
  20.3 1.9 %collective-permute-start.3 = (bf16[256,1024]{1,0:T(8,128)(2,1)}, bf16[256,1024]{1,0:T(8,128)(2,1)S(1)}, u32[]{:S(2)}, u32[]{:S(2)}) collective-permute-start(bf16[256,1024]{1,0:T(8,128)(2,1)} %get-tuple-element.46), channel_id=1, source_target_pairs={{0,1},{1,0},{2,3},{3,2},{4,5},{5,4},{6,7},{7,6},{8,24},{9,25},{10,... | collective-permute-start | bytes 1572872 | tf_op jit(solution)/shard_map/ppermute | solution.py:479
  22.3 0.0 copy-done.3
  22.3 0.0 collective-permute-start.1
  22.3 1.9 %pick_near.1 = (s32[4,4]{1,0:T(4,128)S(1)}, bf16[256,1024]{1,0:T(8,128)(2,1)S(1)}) custom-call(s32[16,16]{1,0:T(8,128)S(1)} %copy-done.2, s32[128]{0:T(128)S(1)} %copy-done.4, bf16[4,256,1024]{2,1,0:T(8,128)(2,1)S(1)} %copy-done), custom_call_target="tpu_custom_call" | custom-call | tf_op jit(solution)/shard_map/pick_near/pallas_call | solution.py:402
  24.2 0.0 collective-permute-done.1.other_pos_ref
  24.2 0.0 collective-permute-done.other_feats_ref
  24.2 0.0 copy-done.1
  24.2 0.1 home.1
  24.3 1.9 %targets.1 = (f32[4,256,256]{2,1,0:T(8,128)S(1)}, f32[3,256,256]{2,1,0:T(8,128)S(1)}, bf16[1,1024,256]{2,1,0:T(8,128)(2,1)S(1)}) custom-call(s32[4,4]{1,0:T(4,128)S(1)} %get-tuple-element.39.table_ref, s32[4,8,128]{2,1,0:T(8,128)S(1)} %get-tuple-element.40.pos_ref, bf16[4,128,1024]{2,1,0:T(8,128)(2,1)S(1)} %get-tuple-element.41.feats_ref), custom_call_target="tpu_custom_call" | custom-call | tf_op jit(solution)/shard_map/targets/pallas_call | solution.py:402
  26.3 1.1 %logits.4 = (f32[1,256,256]{2,1,0:T(8,128)S(1)}, f32[1,3,4,128]{3,2,1,0:T(4,128)S(1)}) custom-call(s32[4,4]{1,0:T(4,128)S(1)} %get-tuple-element.39.table_ref, bf16[4,128,1024]{2,1,0:T(8,128)(2,1)S(1)} %get-tuple-element.41.feats_ref, f32[4,256,256]{2,1,0:T(8,128)S(1)} %get-tuple-element.42.hits_ref, bf16[256,1024]{1,0:T(8,128)(2,1)S(1)} %get-tuple-element.49.rest_0_.rest_4_), custom_call_target="tpu_custom_call" | custom-call | tf_op jit(solution)/shard_map/logits/pallas_call | solution.py:402
  27.4 1.1 %logits.5 = (f32[1,256,256]{2,1,0:T(8,128)S(1)}, f32[1,3,4,128]{3,2,1,0:T(4,128)S(1)}) custom-call(s32[4,4]{1,0:T(4,128)S(1)} %get-tuple-element.39.table_ref, bf16[4,128,1024]{2,1,0:T(8,128)(2,1)S(1)} %get-tuple-element.41.feats_ref, f32[4,256,256]{2,1,0:T(8,128)S(1)} %get-tuple-element.42.hits_ref, ...), custom_call_target="tpu_custom_call" | custom-call | tf_op jit(solution)/shard_map/logits/pallas_call | solution.py:402
  28.5 0.0 collective-permute-done.4.rest_0_.rest_6_
  28.5 1.1 %logits.6 = (f32[1,256,256]{2,1,0:T(8,128)S(1)}, f32[1,3,4,128]{3,2,1,0:T(4,128)S(1)}) custom-call(s32[4,4]{1,0:T(4,128)S(1)} %get-tuple-element.39.table_ref, bf16[4,128,1024]{2,1,0:T(8,128)(2,1)S(1)} %get-tuple-element.41.feats_ref, f32[4,256,256]{2,1,0:T(8,128)S(1)} %get-tuple-element.42.hits_ref, ...), custom_call_target="tpu_custom_call" | custom-call | tf_op jit(solution)/shard_map/logits/pallas_call | solution.py:402
  29.6 1.9 %collective-permute-done.3.rest_0_.rest_7_ = bf16[256,1024]{1,0:T(8,128)(2,1)S(1)} collective-permute-done((bf16[256,1024]{1,0:T(8,128)(2,1)}, bf16[256,1024]{1,0:T(8,128)(2,1)S(1)}, u32[]{:S(2)}, u32[]{:S(2)}) %collective-permute-start.3) | collective-permute-done | bytes 524320 | tf_op jit(solution)/shard_map/ppermute | solution.py:479
  31.5 1.0 %logits.7 = (f32[1,256,256]{2,1,0:T(8,128)S(1)}, f32[8,3,4,128]{3,2,1,0:T(4,128)S(1)}) custom-call(s32[4,4]{1,0:T(4,128)S(1)} %get-tuple-element.39.table_ref, bf16[1,1024,256]{2,1,0:T(8,128)(2,1)S(1)} %get-tuple-element.44.feats_ref, f32[4,256,256]{2,1,0:T(8,128)S(1)} %get-tuple-element.42.hits_ref, ...), custom_call_target="tpu_custom_call" | custom-call | tf_op jit(solution)/shard_map/logits/pallas_call | solution.py:402
  32.4 10.5 %all_to_all.5.stats_ref = f32[8,3,4,128]{3,2,1,0:T(4,128)S(1)} all-to-all(f32[8,3,4,128]{3,2,1,0:T(4,128)S(1)} %get-tuple-element.53), channel_id=1, replica_groups={{0,8,2,10,4,12,6,14},{1,9,3,11,5,13,7,15},{16,24,18,26,20,28,22,30},{17..., dimensions={0} | all-to-all | bytes 98304 | tf_op jit(solution)/shard_map/all_to_all | solution.py:545
  43.0 1.4 %grads.2 = (f32[4,128]{1,0:T(4,128)S(1)}, f32[4,256,128]{2,1,0:T(8,128)S(1)}, bf16[4,256,128]{2,1,0:T(8,128)(2,1)S(1)}) custom-call(s32[4,4]{1,0:T(4,128)S(1)} %get-tuple-element.39.table_ref, f32[4,256,256]{2,1,0:T(8,128)S(1)} %get-tuple-element.42.hits_ref, f32[3,256,256]{2,1,0:T(8,128)S(1)} %get-tuple-element.43.shares_ref, ...), custom_call_target="tpu_custom_call" | custom-call | tf_op jit(solution)/shard_map/grads/pallas_call | solution.py:402
  44.3 0.1 collective-permute-start.10
  44.4 1.8 %grads.3 = (f32[4,128]{1,0:T(4,128)}, f32[4,256,128]{2,1,0:T(8,128)S(1)}, bf16[4,256,128]{2,1,0:T(8,128)(2,1)S(1)}) custom-call(s32[4,4]{1,0:T(4,128)S(1)} %get-tuple-element.39.table_ref, f32[4,256,256]{2,1,0:T(8,128)S(1)} %get-tuple-element.42.hits_ref, f32[3,256,256]{2,1,0:T(8,128)S(1)} %get-tuple-element.43.shares_ref, ...), custom_call_target="tpu_custom_call" | custom-call | tf_op jit(solution)/shard_map/grads/pallas_call | solution.py:402
  46.2 0.5 collective-permute-start.5
  46.7 0.0 collective-permute-done.10.got_ref
  46.8 0.8 %collective-permute-start.11 = (bf16[2,256,128]{2,1,0:T(8,128)(2,1)S(1)}, bf16[2,256,128]{2,1,0:T(8,128)(2,1)S(1)}, u32[]{:S(2)}, u32[]{:S(2)}) collective-permute-start(bf16[2,256,128]{2,1,0:T(8,128)(2,1)S(1)} %get-tuple-element.68), channel_id=1, source_target_pairs={{0,2},{1,3},{2,0},{3,1},{4,6},{5,7},{6,4},{7,5},{8,10},{9,11},{10,... | collective-permute-start | bytes 393224 | tf_op jit(solution)/shard_map/ppermute | solution.py:574
  47.6 0.4 collective-permute-done.5.got_ref
  47.9 0.1 spread_sums.1
  48.0 0.6 collective-permute-start.6
  48.5 2.8 %collective-permute-start.7 = (bf16[256,128]{1,0:T(8,128)(2,1)S(1)}, bf16[256,128]{1,0:T(8,128)(2,1)S(1)}, u32[]{:S(2)}, u32[]{:S(2)}) collective-permute-start(bf16[256,128]{1,0:T(8,128)(2,1)S(1)} %get-tuple-element.63), channel_id=1, source_target_pairs={{0,6},{1,7},{2,4},{3,5},{4,2},{5,3},{6,0},{7,1},{8,14},{9,15},{10,... | collective-permute-start | bytes 196616 | tf_op jit(solution)/shard_map/ppermute | solution.py:574
  51.4 0.2 collective-permute-start.8
  51.5 1.1 %collective-permute-done.11.got_ref = bf16[2,256,128]{2,1,0:T(8,128)(2,1)S(1)} collective-permute-done((bf16[2,256,128]{2,1,0:T(8,128)(2,1)S(1)}, bf16[2,256,128]{2,1,0:T(8,128)(2,1)S(1)}, u32[]{:S(2)}, u32[]{:S(2)}) %collective-permute-start.11) | collective-permute-done | bytes 131104 | tf_op jit(solution)/shard_map/ppermute | solution.py:574
  52.7 0.3 collective-permute-start.12
  53.0 4.2 %collective-permute-done.6.refs_1_ = bf16[256,128]{1,0:T(8,128)(2,1)S(1)} collective-permute-done((bf16[256,128]{1,0:T(8,128)(2,1)S(1)}, bf16[256,128]{1,0:T(8,128)(2,1)S(1)}, u32[]{:S(2)}, u32[]{:S(2)}) %collective-permute-start.6) | collective-permute-done | bytes 65568 | tf_op jit(solution)/shard_map/ppermute | solution.py:574
  57.2 0.0 collective-permute-done.7.refs_2_
  57.2 0.0 collective-permute-done.8.refs_3_
  57.3 1.5 %collective-permute-start.9 = (bf16[272,128]{1,0:T(8,128)(2,1)S(1)}, bf16[272,128]{1,0:T(8,128)(2,1)S(1)}, u32[]{:S(2)}, u32[]{:S(2)}) collective-permute-start(bf16[272,128]{1,0:T(8,128)(2,1)S(1)} %line_sums_loss.1), channel_id=1, source_target_pairs={{0,1},{1,9},{2,3},{3,11},{4,5},{5,13},{6,7},{7,15},{8,0},{9,8},{10... | collective-permute-start | bytes 208904 | tf_op jit(solution)/shard_map/ppermute | solution.py:434
  58.8 1.6 %collective-permute-done.12.refs_1_ = bf16[256,128]{1,0:T(8,128)(2,1)S(1)} collective-permute-done((bf16[256,128]{1,0:T(8,128)(2,1)S(1)}, bf16[256,128]{1,0:T(8,128)(2,1)S(1)}, u32[]{:S(2)}, u32[]{:S(2)}) %collective-permute-start.12) | collective-permute-done | bytes 65568 | tf_op jit(solution)/shard_map/ppermute | solution.py:574
  60.4 1.5 %collective-permute-start.13 = (bf16[256,128]{1,0:T(8,128)(2,1)S(1)}, bf16[256,128]{1,0:T(8,128)(2,1)S(1)}, u32[]{:S(2)}, u32[]{:S(2)}) collective-permute-start(bf16[256,128]{1,0:T(8,128)(2,1)S(1)} %line_sums.1), channel_id=1, source_target_pairs={{0,1},{1,9},{2,3},{3,11},{4,5},{5,13},{6,7},{7,15},{8,0},{9,8},{10... | collective-permute-start | bytes 196616 | tf_op jit(solution)/shard_map/ppermute | solution.py:434
  61.9 0.0 collective-permute-done.9.low_ref
  61.9 1.9 %collective-permute-done.13.high_ref = bf16[256,128]{1,0:T(8,128)(2,1)S(1)} collective-permute-done((bf16[256,128]{1,0:T(8,128)(2,1)S(1)}, bf16[256,128]{1,0:T(8,128)(2,1)S(1)}, u32[]{:S(2)}, u32[]{:S(2)}) %collective-permute-start.13) | collective-permute-done | bytes 65568 | tf_op jit(solution)/shard_map/ppermute | solution.py:434
  63.8 0.7 %home_again.1 = (f32[4,128]{1,0:T(4,128)}, bf16[512,128]{1,0:T(8,128)(2,1)}) custom-call(bf16[272,128]{1,0:T(8,128)(2,1)S(1)} %collective-permute-done.9.low_ref, bf16[256,128]{1,0:T(8,128)(2,1)S(1)} %collective-permute-done.13.high_ref), custom_call_target="tpu_custom_call" | custom-call | tf_op jit(solution)/shard_map/home_again/pallas_call | solution.py:402
  (8 shorter events, 0.1 us)
Async XLA Ops:
  0.6 21.6 %copy-start.3 = (s32[512,8]{0,1:T(8,128)S(1)}, s32[512,8]{0,1:T(8,128)}, u32[]{:S(2)}) copy-start(s32[512,8]{0,1:T(8,128)} %param.9) | copy-start | bytes 49156
  0.6 21.6 %copy-start = (bf16[4,256,1024]{2,1,0:T(8,128)(2,1)S(1)}, bf16[4,256,1024]{2,1,0:T(8,128)(2,1)}, u32[]{:S(2)}) copy-start(bf16[4,256,1024]{2,1,0:T(8,128)(2,1)} %weights_ref.5) | copy-start | bytes 6291460
  0.7 21.6 %copy-start.2 = (s32[16,16]{1,0:T(8,128)S(1)}, s32[16,16]{1,0:T(8,128)}, u32[]{:S(2)}) copy-start(s32[16,16]{1,0:T(8,128)} %lists_hbm.3) | copy-start | bytes 3076
  0.7 21.6 %copy-start.4 = (s32[128]{0:T(128)S(1)}, s32[128]{0:T(128)}, u32[]{:S(2)}) copy-start(s32[128]{0:T(128)} %slot_hbm.3) | copy-start | bytes 1540
  0.7 23.5 %collective-permute-start = (bf16[4,128,1024]{2,1,0:T(8,128)(2,1)}, bf16[4,128,1024]{2,1,0:T(8,128)(2,1)S(1)}, u32[]{:S(2)}, u32[]{:S(2)}) collective-permute-start(bf16[4,128,1024]{2,1,0:T(8,128)(2,1)} %bitcast.5), channel_id=1, source_target_pairs={{0,8},{8,0},{16,24},{24,16},{1,9},{9,1},{17,25},{25,17},{2,10},{10... | collective-permute-start | bytes 3145736 | tf_op jit(solution)/shard_map/ppermute | solution.py:439
  3.7 20.4 %copy-start.1 = (bf16[512,1024]{1,0:T(8,128)(2,1)S(1)}, bf16[512,1024]{1,0:T(8,128)(2,1)}, u32[]{:S(2)}) copy-start(bf16[512,1024]{1,0:T(8,128)(2,1)} %param.5) | copy-start | bytes 3145732
  3.8 16.6 %collective-permute-start.2 = (bf16[256,1024]{1,0:T(8,128)(2,1)}, bf16[256,1024]{1,0:T(8,128)(2,1)S(1)}, u32[]{:S(2)}, u32[]{:S(2)}) collective-permute-start(bf16[256,1024]{1,0:T(8,128)(2,1)} %pick_far.3), channel_id=1, source_target_pairs={{0,17},{1,16},{2,19},{3,18},{4,21},{5,20},{6,23},{7,22},{8,25},{9,... | collective-permute-start | bytes 1572872 | tf_op jit(solution)/shard_map/ppermute | solution.py:479
  9.9 18.6 %collective-permute-start.4 = (bf16[256,1024]{1,0:T(8,128)(2,1)}, bf16[256,1024]{1,0:T(8,128)(2,1)S(1)}, u32[]{:S(2)}, u32[]{:S(2)}) collective-permute-start(bf16[256,1024]{1,0:T(8,128)(2,1)} %get-tuple-element.47), channel_id=1, source_target_pairs={{0,16},{1,17},{2,18},{3,19},{4,20},{5,21},{6,22},{7,23},{8,9},{9,8... | collective-permute-start | bytes 1572872 | tf_op jit(solution)/shard_map/ppermute | solution.py:479
  20.3 11.2 %collective-permute-start.3 = (bf16[256,1024]{1,0:T(8,128)(2,1)}, bf16[256,1024]{1,0:T(8,128)(2,1)S(1)}, u32[]{:S(2)}, u32[]{:S(2)}) collective-permute-start(bf16[256,1024]{1,0:T(8,128)(2,1)} %get-tuple-element.46), channel_id=1, source_target_pairs={{0,1},{1,0},{2,3},{3,2},{4,5},{5,4},{6,7},{7,6},{8,24},{9,25},{10,... | collective-permute-start | bytes 1572872 | tf_op jit(solution)/shard_map/ppermute | solution.py:479
  22.3 1.9 %collective-permute-start.1 = (s32[4,8,128]{2,1,0:T(8,128)S(1)}, s32[4,8,128]{2,1,0:T(8,128)S(1)}, u32[]{:S(2)}, u32[]{:S(2)}) collective-permute-start(s32[4,8,128]{2,1,0:T(8,128)S(1)} %bitcast.7), channel_id=1, source_target_pairs={{0,8},{8,0},{16,24},{24,16},{1,9},{9,1},{17,25},{25,17},{2,10},{10... | collective-permute-start | bytes 49160 | tf_op jit(solution)/shard_map/ppermute | solution.py:440
  44.3 2.4 %collective-permute-start.10 = (bf16[4,256,128]{2,1,0:T(8,128)(2,1)S(1)}, bf16[4,256,128]{2,1,0:T(8,128)(2,1)S(1)}, u32[]{:S(2)}, u32[]{:S(2)}) collective-permute-start(bf16[4,256,128]{2,1,0:T(8,128)(2,1)S(1)} %get-tuple-element.66), channel_id=1, source_target_pairs={{0,8},{8,0},{16,24},{24,16},{1,9},{9,1},{17,25},{25,17},{2,10},{10... | collective-permute-start | bytes 786440 | tf_op jit(solution)/shard_map/ppermute | solution.py:571
  46.2 1.7 %collective-permute-start.5 = (bf16[4,256,128]{2,1,0:T(8,128)(2,1)S(1)}, bf16[4,256,128]{2,1,0:T(8,128)(2,1)S(1)}, u32[]{:S(2)}, u32[]{:S(2)}) collective-permute-start(bf16[4,256,128]{2,1,0:T(8,128)(2,1)S(1)} %get-tuple-element.60), channel_id=1, source_target_pairs={{0,8},{8,0},{16,24},{24,16},{1,9},{9,1},{17,25},{25,17},{2,10},{10... | collective-permute-start | bytes 786440 | tf_op jit(solution)/shard_map/ppermute | solution.py:571
  46.8 5.9 %collective-permute-start.11 = (bf16[2,256,128]{2,1,0:T(8,128)(2,1)S(1)}, bf16[2,256,128]{2,1,0:T(8,128)(2,1)S(1)}, u32[]{:S(2)}, u32[]{:S(2)}) collective-permute-start(bf16[2,256,128]{2,1,0:T(8,128)(2,1)S(1)} %get-tuple-element.68), channel_id=1, source_target_pairs={{0,2},{1,3},{2,0},{3,1},{4,6},{5,7},{6,4},{7,5},{8,10},{9,11},{10,... | collective-permute-start | bytes 393224 | tf_op jit(solution)/shard_map/ppermute | solution.py:574
  48.0 9.2 %collective-permute-start.6 = (bf16[256,128]{1,0:T(8,128)(2,1)S(1)}, bf16[256,128]{1,0:T(8,128)(2,1)S(1)}, u32[]{:S(2)}, u32[]{:S(2)}) collective-permute-start(bf16[256,128]{1,0:T(8,128)(2,1)S(1)} %get-tuple-element.62), channel_id=1, source_target_pairs={{0,4},{1,5},{2,6},{3,7},{4,0},{5,1},{6,2},{7,3},{8,12},{9,13},{10,... | collective-permute-start | bytes 196616 | tf_op jit(solution)/shard_map/ppermute | solution.py:574
  48.5 8.7 %collective-permute-start.7 = (bf16[256,128]{1,0:T(8,128)(2,1)S(1)}, bf16[256,128]{1,0:T(8,128)(2,1)S(1)}, u32[]{:S(2)}, u32[]{:S(2)}) collective-permute-start(bf16[256,128]{1,0:T(8,128)(2,1)S(1)} %get-tuple-element.63), channel_id=1, source_target_pairs={{0,6},{1,7},{2,4},{3,5},{4,2},{5,3},{6,0},{7,1},{8,14},{9,15},{10,... | collective-permute-start | bytes 196616 | tf_op jit(solution)/shard_map/ppermute | solution.py:574
  51.4 5.8 %collective-permute-start.8 = (bf16[256,128]{1,0:T(8,128)(2,1)S(1)}, bf16[256,128]{1,0:T(8,128)(2,1)S(1)}, u32[]{:S(2)}, u32[]{:S(2)}) collective-permute-start(bf16[256,128]{1,0:T(8,128)(2,1)S(1)} %get-tuple-element.64), channel_id=1, source_target_pairs={{0,2},{1,3},{2,0},{3,1},{4,6},{5,7},{6,4},{7,5},{8,10},{9,11},{10,... | collective-permute-start | bytes 196616 | tf_op jit(solution)/shard_map/ppermute | solution.py:574
  52.7 7.7 %collective-permute-start.12 = (bf16[256,128]{1,0:T(8,128)(2,1)S(1)}, bf16[256,128]{1,0:T(8,128)(2,1)S(1)}, u32[]{:S(2)}, u32[]{:S(2)}) collective-permute-start(bf16[256,128]{1,0:T(8,128)(2,1)S(1)} %get-tuple-element.71), channel_id=1, source_target_pairs={{0,4},{1,5},{2,6},{3,7},{4,0},{5,1},{6,2},{7,3},{8,12},{9,13},{10,... | collective-permute-start | bytes 196616 | tf_op jit(solution)/shard_map/ppermute | solution.py:574
  57.3 4.6 %collective-permute-start.9 = (bf16[272,128]{1,0:T(8,128)(2,1)S(1)}, bf16[272,128]{1,0:T(8,128)(2,1)S(1)}, u32[]{:S(2)}, u32[]{:S(2)}) collective-permute-start(bf16[272,128]{1,0:T(8,128)(2,1)S(1)} %line_sums_loss.1), channel_id=1, source_target_pairs={{0,1},{1,9},{2,3},{3,11},{4,5},{5,13},{6,7},{7,15},{8,0},{9,8},{10... | collective-permute-start | bytes 208904 | tf_op jit(solution)/shard_map/ppermute | solution.py:434
  60.4 3.4 %collective-permute-start.13 = (bf16[256,128]{1,0:T(8,128)(2,1)S(1)}, bf16[256,128]{1,0:T(8,128)(2,1)S(1)}, u32[]{:S(2)}, u32[]{:S(2)}) collective-permute-start(bf16[256,128]{1,0:T(8,128)(2,1)S(1)} %line_sums.1), channel_id=1, source_target_pairs={{0,1},{1,9},{2,3},{3,11},{4,5},{5,13},{6,7},{7,15},{8,0},{9,8},{10... | collective-permute-start | bytes 196616 | tf_op jit(solution)/shard_map/ppermute | solution.py:434

commit v4 on v2

--- a/solution.py
+++ b/solution.py
@@ -47,7 +47,7 @@
         return (dp & ~1) | (lab & 1) if self.square else dp
 
     def flips(self, entry, core):
-        return [(0, 0), (1, 1), (core, 1 - core), (1 - core, core)][entry]
+        return [(0, 0), (1, 1), (1 - core, core), (core, 1 - core)][entry]
 
     def wanted_by(self, entry):
         dp, lab = self.here()
@@ -64,7 +64,7 @@
         match = ((that_dp & 1) == (dp & 1)) & ((that_lab >> 1) == (lab >> 1))
         flip_y, flip_x = (that_dp ^ dp) >> 1, (that_lab ^ lab) & 1
         core = dp & 1
-        lone = jnp.where(flip_y == 1 - core, 2, 3)
+        lone = jnp.where(flip_y == core, 2, 3)
         entry = jnp.where(flip_x + flip_y == 1, lone, (flip_x + flip_y) >> 1)
         return match, entry
 

time: 64 us -> 63.9 us (level)
  transfers between devices with their start and end apart: 14 -> 14, of which waited for: 7 -> 8; matrix products, arithmetic and copies ran while one was open for 0% -> 0% of each run, Pallas kernels for 23% -> 23%
where the time goes in v4:
time: 63.9 us; the launch traced here: 63.7 us
  waiting for transfers between devices  19.8 us (31%)
  Pallas kernels  17.4 us (27%)
  starting transfers between devices  15 us (23%)
  blocking collectives  10.7 us (17%)
  between operations  0.8 us (1%)
    pallas_call x17, Pallas kernels, call(): pl.pallas_call(kernel, out_shape=out_shape, in_specs=in_specs, out_specs=...  17.4 us
    ppermute x3, waiting for transfers between devices, shards(): rows.append(lax.ppermute(x, both, plan.pairs(k)))  11.6 us
    all_to_all x1, blocking collectives, shards(): lax.all_to_all(stats[0], both, split_axis=0, concat_axis=0, axis_index_gr...  10.7 us
    ppermute x5, waiting for transfers between devices, hop(): return lax.ppermute(x, 'label', [(i, i ^ mask) for i in range(lab_count)])  5.93 us
    ppermute x3, starting transfers between devices, shards(): rows.append(lax.ppermute(x, both, plan.pairs(k)))  5.87 us
    ppermute x5, starting transfers between devices, hop(): return lax.ppermute(x, 'label', [(i, i ^ mask) for i in range(lab_count)])  5.61 us
    ppermute x2, starting transfers between devices, move(): return lax.ppermute(x, both, pairs)  2.42 us
    ppermute x2, waiting for transfers between devices, move(): return lax.ppermute(x, both, pairs)  1.91 us
  transfers between devices with their start and end apart: 14, of which 8 were waited for; matrix products, arithmetic and copies ran while one was open for 0% of the time, Pallas kernels for 23%

profile of v4, /device:TPU:0, one launch (start us, length us, event | category | flops | bytes accessed | tf_op | source)
XLA Modules:
  0.0 63.7 jit_solution(6082472173046347096)
XLA Ops:
  0.6 0.0 copy-start.3
  0.6 0.0 copy-start
  0.7 0.0 copy-start.2
  0.7 0.0 copy-start.4
  0.7 0.5 collective-permute-start
  1.2 2.5 %pick_far.3 = bf16[256,1024]{1,0:T(8,128)(2,1)} custom-call(s32[16,16]{1,0:T(8,128)} %lists_hbm.3, s32[128]{0:T(128)} %slot_hbm.3, bf16[4,256,1024]{2,1,0:T(8,128)(2,1)} %weights_ref.5), custom_call_target="tpu_custom_call" | custom-call | tf_op jit(solution)/shard_map/pick_far/pallas_call | solution.py:402
  3.7 0.0 copy-start.1
  3.8 3.6 %collective-permute-start.2 = (bf16[256,1024]{1,0:T(8,128)(2,1)}, bf16[256,1024]{1,0:T(8,128)(2,1)S(1)}, u32[]{:S(2)}, u32[]{:S(2)}) collective-permute-start(bf16[256,1024]{1,0:T(8,128)(2,1)} %pick_far.3), channel_id=1, source_target_pairs={{0,17},{1,16},{2,19},{3,18},{4,21},{5,20},{6,23},{7,22},{8,25},{9,... | collective-permute-start | bytes 1572872 | tf_op jit(solution)/shard_map/ppermute | solution.py:479
  7.3 2.6 %pick_far.2 = (bf16[256,1024]{1,0:T(8,128)(2,1)}, bf16[256,1024]{1,0:T(8,128)(2,1)}) custom-call(s32[16,16]{1,0:T(8,128)} %lists_hbm.3, s32[128]{0:T(128)} %slot_hbm.3, bf16[4,256,1024]{2,1,0:T(8,128)(2,1)} %weights_ref.5), custom_call_target="tpu_custom_call" | custom-call | tf_op jit(solution)/shard_map/pick_far/pallas_call | solution.py:402
  9.9 0.6 collective-permute-start.4
  10.5 9.5 %collective-permute-done.2.rest_0_.rest_5_ = bf16[256,1024]{1,0:T(8,128)(2,1)S(1)} collective-permute-done((bf16[256,1024]{1,0:T(8,128)(2,1)}, bf16[256,1024]{1,0:T(8,128)(2,1)S(1)}, u32[]{:S(2)}, u32[]{:S(2)}) %collective-permute-start.2) | collective-permute-done | bytes 524320 | tf_op jit(solution)/shard_map/ppermute | solution.py:479
  20.1 1.7 %collective-permute-start.3 = (bf16[256,1024]{1,0:T(8,128)(2,1)}, bf16[256,1024]{1,0:T(8,128)(2,1)S(1)}, u32[]{:S(2)}, u32[]{:S(2)}) collective-permute-start(bf16[256,1024]{1,0:T(8,128)(2,1)} %get-tuple-element.46), channel_id=1, source_target_pairs={{0,16},{1,17},{2,18},{3,19},{4,20},{5,21},{6,22},{7,23},{8,9},{9,8... | collective-permute-start | bytes 1572872 | tf_op jit(solution)/shard_map/ppermute | solution.py:479
  21.8 0.0 collective-permute-start.1
  21.8 1.9 %pick_near.1 = (s32[4,4]{1,0:T(4,128)S(1)}, bf16[256,1024]{1,0:T(8,128)(2,1)S(1)}) custom-call(s32[16,16]{1,0:T(8,128)S(1)} %copy-done.2, s32[128]{0:T(128)S(1)} %copy-done.4, bf16[4,256,1024]{2,1,0:T(8,128)(2,1)S(1)} %copy-done), custom_call_target="tpu_custom_call" | custom-call | tf_op jit(solution)/shard_map/pick_near/pallas_call | solution.py:402
  23.7 0.0 collective-permute-done.1.other_pos_ref
  23.7 0.0 collective-permute-done.other_feats_ref
  23.7 0.0 copy-done.1
  23.7 0.1 home.1
  23.8 1.9 %targets.1 = (f32[4,256,256]{2,1,0:T(8,128)S(1)}, f32[3,256,256]{2,1,0:T(8,128)S(1)}, bf16[1,1024,256]{2,1,0:T(8,128)(2,1)S(1)}) custom-call(s32[4,4]{1,0:T(4,128)S(1)} %get-tuple-element.39.table_ref, s32[4,8,128]{2,1,0:T(8,128)S(1)} %get-tuple-element.40.pos_ref, bf16[4,128,1024]{2,1,0:T(8,128)(2,1)S(1)} %get-tuple-element.41.feats_ref), custom_call_target="tpu_custom_call" | custom-call | tf_op jit(solution)/shard_map/targets/pallas_call | solution.py:402
  25.8 1.1 %logits.4 = (f32[1,256,256]{2,1,0:T(8,128)S(1)}, f32[1,3,4,128]{3,2,1,0:T(4,128)S(1)}) custom-call(s32[4,4]{1,0:T(4,128)S(1)} %get-tuple-element.39.table_ref, bf16[4,128,1024]{2,1,0:T(8,128)(2,1)S(1)} %get-tuple-element.41.feats_ref, f32[4,256,256]{2,1,0:T(8,128)S(1)} %get-tuple-element.42.hits_ref, bf16[256,1024]{1,0:T(8,128)(2,1)S(1)} %get-tuple-element.49.rest_0_.rest_4_), custom_call_target="tpu_custom_call" | custom-call | tf_op jit(solution)/shard_map/logits/pallas_call | solution.py:402
  26.9 1.1 %logits.5 = (f32[1,256,256]{2,1,0:T(8,128)S(1)}, f32[1,3,4,128]{3,2,1,0:T(4,128)S(1)}) custom-call(s32[4,4]{1,0:T(4,128)S(1)} %get-tuple-element.39.table_ref, bf16[4,128,1024]{2,1,0:T(8,128)(2,1)S(1)} %get-tuple-element.41.feats_ref, f32[4,256,256]{2,1,0:T(8,128)S(1)} %get-tuple-element.42.hits_ref, ...), custom_call_target="tpu_custom_call" | custom-call | tf_op jit(solution)/shard_map/logits/pallas_call | solution.py:402
  28.0 1.1 %collective-permute-done.4.rest_0_.rest_6_ = bf16[256,1024]{1,0:T(8,128)(2,1)S(1)} collective-permute-done((bf16[256,1024]{1,0:T(8,128)(2,1)}, bf16[256,1024]{1,0:T(8,128)(2,1)S(1)}, u32[]{:S(2)}, u32[]{:S(2)}) %collective-permute-start.4) | collective-permute-done | bytes 524320 | tf_op jit(solution)/shard_map/ppermute | solution.py:479
  29.1 1.1 %logits.6 = (f32[1,256,256]{2,1,0:T(8,128)S(1)}, f32[1,3,4,128]{3,2,1,0:T(4,128)S(1)}) custom-call(s32[4,4]{1,0:T(4,128)S(1)} %get-tuple-element.39.table_ref, bf16[4,128,1024]{2,1,0:T(8,128)(2,1)S(1)} %get-tuple-element.41.feats_ref, f32[4,256,256]{2,1,0:T(8,128)S(1)} %get-tuple-element.42.hits_ref, ...), custom_call_target="tpu_custom_call" | custom-call | tf_op jit(solution)/shard_map/logits/pallas_call | solution.py:402
  30.2 1.0 %collective-permute-done.3.rest_0_.rest_7_ = bf16[256,1024]{1,0:T(8,128)(2,1)S(1)} collective-permute-done((bf16[256,1024]{1,0:T(8,128)(2,1)}, bf16[256,1024]{1,0:T(8,128)(2,1)S(1)}, u32[]{:S(2)}, u32[]{:S(2)}) %collective-permute-start.3) | collective-permute-done | bytes 524320 | tf_op jit(solution)/shard_map/ppermute | solution.py:479
  31.2 1.0 %logits.7 = (f32[1,256,256]{2,1,0:T(8,128)S(1)}, f32[8,3,4,128]{3,2,1,0:T(4,128)S(1)}) custom-call(s32[4,4]{1,0:T(4,128)S(1)} %get-tuple-element.39.table_ref, bf16[1,1024,256]{2,1,0:T(8,128)(2,1)S(1)} %get-tuple-element.44.feats_ref, f32[4,256,256]{2,1,0:T(8,128)S(1)} %get-tuple-element.42.hits_ref, ...), custom_call_target="tpu_custom_call" | custom-call | tf_op jit(solution)/shard_map/logits/pallas_call | solution.py:402
  32.2 10.7 %all_to_all.5.stats_ref = f32[8,3,4,128]{3,2,1,0:T(4,128)S(1)} all-to-all(f32[8,3,4,128]{3,2,1,0:T(4,128)S(1)} %get-tuple-element.53), channel_id=1, replica_groups={{0,8,2,10,4,12,6,14},{1,9,3,11,5,13,7,15},{16,24,18,26,20,28,22,30},{17..., dimensions={0} | all-to-all | bytes 98304 | tf_op jit(solution)/shard_map/all_to_all | solution.py:545
  42.9 1.4 %grads.2 = (f32[4,128]{1,0:T(4,128)S(1)}, f32[4,256,128]{2,1,0:T(8,128)S(1)}, bf16[4,256,128]{2,1,0:T(8,128)(2,1)S(1)}) custom-call(s32[4,4]{1,0:T(4,128)S(1)} %get-tuple-element.39.table_ref, f32[4,256,256]{2,1,0:T(8,128)S(1)} %get-tuple-element.42.hits_ref, f32[3,256,256]{2,1,0:T(8,128)S(1)} %get-tuple-element.43.shares_ref, ...), custom_call_target="tpu_custom_call" | custom-call | tf_op jit(solution)/shard_map/grads/pallas_call | solution.py:402
  44.2 0.1 collective-permute-start.10
  44.3 1.8 %grads.3 = (f32[4,128]{1,0:T(4,128)}, f32[4,256,128]{2,1,0:T(8,128)S(1)}, bf16[4,256,128]{2,1,0:T(8,128)(2,1)S(1)}) custom-call(s32[4,4]{1,0:T(4,128)S(1)} %get-tuple-element.39.table_ref, f32[4,256,256]{2,1,0:T(8,128)S(1)} %get-tuple-element.42.hits_ref, f32[3,256,256]{2,1,0:T(8,128)S(1)} %get-tuple-element.43.shares_ref, ...), custom_call_target="tpu_custom_call" | custom-call | tf_op jit(solution)/shard_map/grads/pallas_call | solution.py:402
  46.1 0.5 collective-permute-start.5
  46.6 0.0 collective-permute-done.10.got_ref
  46.7 0.8 %collective-permute-start.11 = (bf16[2,256,128]{2,1,0:T(8,128)(2,1)S(1)}, bf16[2,256,128]{2,1,0:T(8,128)(2,1)S(1)}, u32[]{:S(2)}, u32[]{:S(2)}) collective-permute-start(bf16[2,256,128]{2,1,0:T(8,128)(2,1)S(1)} %get-tuple-element.68), channel_id=1, source_target_pairs={{0,2},{1,3},{2,0},{3,1},{4,6},{5,7},{6,4},{7,5},{8,10},{9,11},{10,... | collective-permute-start | bytes 393224 | tf_op jit(solution)/shard_map/ppermute | solution.py:574
  47.5 0.4 collective-permute-done.5.got_ref
  47.8 0.1 spread_sums.1
  47.9 1.0 %collective-permute-start.6 = (bf16[256,128]{1,0:T(8,128)(2,1)S(1)}, bf16[256,128]{1,0:T(8,128)(2,1)S(1)}, u32[]{:S(2)}, u32[]{:S(2)}) collective-permute-start(bf16[256,128]{1,0:T(8,128)(2,1)S(1)} %get-tuple-element.62), channel_id=1, source_target_pairs={{0,6},{1,7},{2,4},{3,5},{4,2},{5,3},{6,0},{7,1},{8,14},{9,15},{10,... | collective-permute-start | bytes 196616 | tf_op jit(solution)/shard_map/ppermute | solution.py:574
  48.8 1.5 %collective-permute-start.7 = (bf16[256,128]{1,0:T(8,128)(2,1)S(1)}, bf16[256,128]{1,0:T(8,128)(2,1)S(1)}, u32[]{:S(2)}, u32[]{:S(2)}) collective-permute-start(bf16[256,128]{1,0:T(8,128)(2,1)S(1)} %get-tuple-element.63), channel_id=1, source_target_pairs={{0,4},{1,5},{2,6},{3,7},{4,0},{5,1},{6,2},{7,3},{8,12},{9,13},{10,... | collective-permute-start | bytes 196616 | tf_op jit(solution)/shard_map/ppermute | solution.py:574
  50.4 2.0 %collective-permute-start.8 = (bf16[256,128]{1,0:T(8,128)(2,1)S(1)}, bf16[256,128]{1,0:T(8,128)(2,1)S(1)}, u32[]{:S(2)}, u32[]{:S(2)}) collective-permute-start(bf16[256,128]{1,0:T(8,128)(2,1)S(1)} %get-tuple-element.64), channel_id=1, source_target_pairs={{0,2},{1,3},{2,0},{3,1},{4,6},{5,7},{6,4},{7,5},{8,10},{9,11},{10,... | collective-permute-start | bytes 196616 | tf_op jit(solution)/shard_map/ppermute | solution.py:574
  52.3 0.0 collective-permute-done.11.got_ref
  52.4 0.4 collective-permute-start.12
  52.8 2.0 %collective-permute-done.6.refs_1_ = bf16[256,128]{1,0:T(8,128)(2,1)S(1)} collective-permute-done((bf16[256,128]{1,0:T(8,128)(2,1)S(1)}, bf16[256,128]{1,0:T(8,128)(2,1)S(1)}, u32[]{:S(2)}, u32[]{:S(2)}) %collective-permute-start.6) | collective-permute-done | bytes 65568 | tf_op jit(solution)/shard_map/ppermute | solution.py:574
  54.8 3.9 %collective-permute-done.7.refs_2_ = bf16[256,128]{1,0:T(8,128)(2,1)S(1)} collective-permute-done((bf16[256,128]{1,0:T(8,128)(2,1)S(1)}, bf16[256,128]{1,0:T(8,128)(2,1)S(1)}, u32[]{:S(2)}, u32[]{:S(2)}) %collective-permute-start.7) | collective-permute-done | bytes 65568 | tf_op jit(solution)/shard_map/ppermute | solution.py:574
  58.7 0.0 collective-permute-done.8.refs_3_
  58.7 1.5 %collective-permute-start.9 = (bf16[272,128]{1,0:T(8,128)(2,1)S(1)}, bf16[272,128]{1,0:T(8,128)(2,1)S(1)}, u32[]{:S(2)}, u32[]{:S(2)}) collective-permute-start(bf16[272,128]{1,0:T(8,128)(2,1)S(1)} %line_sums_loss.1), channel_id=1, source_target_pairs={{0,1},{1,9},{2,3},{3,11},{4,5},{5,13},{6,7},{7,15},{8,0},{9,8},{10... | collective-permute-start | bytes 208904 | tf_op jit(solution)/shard_map/ppermute | solution.py:434
  60.2 0.0 collective-permute-done.12.refs_1_
  60.3 0.9 %collective-permute-start.13 = (bf16[256,128]{1,0:T(8,128)(2,1)S(1)}, bf16[256,128]{1,0:T(8,128)(2,1)S(1)}, u32[]{:S(2)}, u32[]{:S(2)}) collective-permute-start(bf16[256,128]{1,0:T(8,128)(2,1)S(1)} %line_sums.1), channel_id=1, source_target_pairs={{0,1},{1,9},{2,3},{3,11},{4,5},{5,13},{6,7},{7,15},{8,0},{9,8},{10... | collective-permute-start | bytes 196616 | tf_op jit(solution)/shard_map/ppermute | solution.py:434
  61.2 1.0 %collective-permute-done.9.low_ref = bf16[272,128]{1,0:T(8,128)(2,1)S(1)} collective-permute-done((bf16[272,128]{1,0:T(8,128)(2,1)S(1)}, bf16[272,128]{1,0:T(8,128)(2,1)S(1)}, u32[]{:S(2)}, u32[]{:S(2)}) %collective-permute-start.9) | collective-permute-done | bytes 69664 | tf_op jit(solution)/shard_map/ppermute | solution.py:434
  62.2 0.9 %collective-permute-done.13.high_ref = bf16[256,128]{1,0:T(8,128)(2,1)S(1)} collective-permute-done((bf16[256,128]{1,0:T(8,128)(2,1)S(1)}, bf16[256,128]{1,0:T(8,128)(2,1)S(1)}, u32[]{:S(2)}, u32[]{:S(2)}) %collective-permute-start.13) | collective-permute-done | bytes 65568 | tf_op jit(solution)/shard_map/ppermute | solution.py:434
  63.1 0.7 %home_again.1 = (f32[4,128]{1,0:T(4,128)}, bf16[512,128]{1,0:T(8,128)(2,1)}) custom-call(bf16[272,128]{1,0:T(8,128)(2,1)S(1)} %collective-permute-done.9.low_ref, bf16[256,128]{1,0:T(8,128)(2,1)S(1)} %collective-permute-done.13.high_ref), custom_call_target="tpu_custom_call" | custom-call | tf_op jit(solution)/shard_map/home_again/pallas_call | solution.py:402
  (8 shorter events, 0.1 us)
Async XLA Ops:
  0.6 21.2 %copy-start.3 = (s32[512,8]{0,1:T(8,128)S(1)}, s32[512,8]{0,1:T(8,128)}, u32[]{:S(2)}) copy-start(s32[512,8]{0,1:T(8,128)} %param.9) | copy-start | bytes 49156
  0.6 21.1 %copy-start = (bf16[4,256,1024]{2,1,0:T(8,128)(2,1)S(1)}, bf16[4,256,1024]{2,1,0:T(8,128)(2,1)}, u32[]{:S(2)}) copy-start(bf16[4,256,1024]{2,1,0:T(8,128)(2,1)} %weights_ref.5) | copy-start | bytes 6291460
  0.7 21.1 %copy-start.2 = (s32[16,16]{1,0:T(8,128)S(1)}, s32[16,16]{1,0:T(8,128)}, u32[]{:S(2)}) copy-start(s32[16,16]{1,0:T(8,128)} %lists_hbm.3) | copy-start | bytes 3076
  0.7 21.1 %copy-start.4 = (s32[128]{0:T(128)S(1)}, s32[128]{0:T(128)}, u32[]{:S(2)}) copy-start(s32[128]{0:T(128)} %slot_hbm.3) | copy-start | bytes 1540
  0.7 23.0 %collective-permute-start = (bf16[4,128,1024]{2,1,0:T(8,128)(2,1)}, bf16[4,128,1024]{2,1,0:T(8,128)(2,1)S(1)}, u32[]{:S(2)}, u32[]{:S(2)}) collective-permute-start(bf16[4,128,1024]{2,1,0:T(8,128)(2,1)} %bitcast.5), channel_id=1, source_target_pairs={{0,8},{8,0},{16,24},{24,16},{1,9},{9,1},{17,25},{25,17},{2,10},{10... | collective-permute-start | bytes 3145736 | tf_op jit(solution)/shard_map/ppermute | solution.py:439
  3.7 20.0 %copy-start.1 = (bf16[512,1024]{1,0:T(8,128)(2,1)S(1)}, bf16[512,1024]{1,0:T(8,128)(2,1)}, u32[]{:S(2)}) copy-start(bf16[512,1024]{1,0:T(8,128)(2,1)} %param.5) | copy-start | bytes 3145732
  3.8 16.3 %collective-permute-start.2 = (bf16[256,1024]{1,0:T(8,128)(2,1)}, bf16[256,1024]{1,0:T(8,128)(2,1)S(1)}, u32[]{:S(2)}, u32[]{:S(2)}) collective-permute-start(bf16[256,1024]{1,0:T(8,128)(2,1)} %pick_far.3), channel_id=1, source_target_pairs={{0,17},{1,16},{2,19},{3,18},{4,21},{5,20},{6,23},{7,22},{8,25},{9,... | collective-permute-start | bytes 1572872 | tf_op jit(solution)/shard_map/ppermute | solution.py:479
  9.9 19.1 %collective-permute-start.4 = (bf16[256,1024]{1,0:T(8,128)(2,1)}, bf16[256,1024]{1,0:T(8,128)(2,1)S(1)}, u32[]{:S(2)}, u32[]{:S(2)}) collective-permute-start(bf16[256,1024]{1,0:T(8,128)(2,1)} %get-tuple-element.47), channel_id=1, source_target_pairs={{0,1},{1,0},{2,3},{3,2},{4,5},{5,4},{6,7},{7,6},{8,24},{9,25},{10,... | collective-permute-start | bytes 1572872 | tf_op jit(solution)/shard_map/ppermute | solution.py:479
  20.1 11.1 %collective-permute-start.3 = (bf16[256,1024]{1,0:T(8,128)(2,1)}, bf16[256,1024]{1,0:T(8,128)(2,1)S(1)}, u32[]{:S(2)}, u32[]{:S(2)}) collective-permute-start(bf16[256,1024]{1,0:T(8,128)(2,1)} %get-tuple-element.46), channel_id=1, source_target_pairs={{0,16},{1,17},{2,18},{3,19},{4,20},{5,21},{6,22},{7,23},{8,9},{9,8... | collective-permute-start | bytes 1572872 | tf_op jit(solution)/shard_map/ppermute | solution.py:479
  21.8 1.9 %collective-permute-start.1 = (s32[4,8,128]{2,1,0:T(8,128)S(1)}, s32[4,8,128]{2,1,0:T(8,128)S(1)}, u32[]{:S(2)}, u32[]{:S(2)}) collective-permute-start(s32[4,8,128]{2,1,0:T(8,128)S(1)} %bitcast.7), channel_id=1, source_target_pairs={{0,8},{8,0},{16,24},{24,16},{1,9},{9,1},{17,25},{25,17},{2,10},{10... | collective-permute-start | bytes 49160 | tf_op jit(solution)/shard_map/ppermute | solution.py:440
  44.2 2.4 %collective-permute-start.10 = (bf16[4,256,128]{2,1,0:T(8,128)(2,1)S(1)}, bf16[4,256,128]{2,1,0:T(8,128)(2,1)S(1)}, u32[]{:S(2)}, u32[]{:S(2)}) collective-permute-start(bf16[4,256,128]{2,1,0:T(8,128)(2,1)S(1)} %get-tuple-element.66), channel_id=1, source_target_pairs={{0,8},{8,0},{16,24},{24,16},{1,9},{9,1},{17,25},{25,17},{2,10},{10... | collective-permute-start | bytes 786440 | tf_op jit(solution)/shard_map/ppermute | solution.py:571
  46.1 1.7 %collective-permute-start.5 = (bf16[4,256,128]{2,1,0:T(8,128)(2,1)S(1)}, bf16[4,256,128]{2,1,0:T(8,128)(2,1)S(1)}, u32[]{:S(2)}, u32[]{:S(2)}) collective-permute-start(bf16[4,256,128]{2,1,0:T(8,128)(2,1)S(1)} %get-tuple-element.60), channel_id=1, source_target_pairs={{0,8},{8,0},{16,24},{24,16},{1,9},{9,1},{17,25},{25,17},{2,10},{10... | collective-permute-start | bytes 786440 | tf_op jit(solution)/shard_map/ppermute | solution.py:571
  46.7 5.7 %collective-permute-start.11 = (bf16[2,256,128]{2,1,0:T(8,128)(2,1)S(1)}, bf16[2,256,128]{2,1,0:T(8,128)(2,1)S(1)}, u32[]{:S(2)}, u32[]{:S(2)}) collective-permute-start(bf16[2,256,128]{2,1,0:T(8,128)(2,1)S(1)} %get-tuple-element.68), channel_id=1, source_target_pairs={{0,2},{1,3},{2,0},{3,1},{4,6},{5,7},{6,4},{7,5},{8,10},{9,11},{10,... | collective-permute-start | bytes 393224 | tf_op jit(solution)/shard_map/ppermute | solution.py:574
  47.9 6.9 %collective-permute-start.6 = (bf16[256,128]{1,0:T(8,128)(2,1)S(1)}, bf16[256,128]{1,0:T(8,128)(2,1)S(1)}, u32[]{:S(2)}, u32[]{:S(2)}) collective-permute-start(bf16[256,128]{1,0:T(8,128)(2,1)S(1)} %get-tuple-element.62), channel_id=1, source_target_pairs={{0,6},{1,7},{2,4},{3,5},{4,2},{5,3},{6,0},{7,1},{8,14},{9,15},{10,... | collective-permute-start | bytes 196616 | tf_op jit(solution)/shard_map/ppermute | solution.py:574
  48.8 9.8 %collective-permute-start.7 = (bf16[256,128]{1,0:T(8,128)(2,1)S(1)}, bf16[256,128]{1,0:T(8,128)(2,1)S(1)}, u32[]{:S(2)}, u32[]{:S(2)}) collective-permute-start(bf16[256,128]{1,0:T(8,128)(2,1)S(1)} %get-tuple-element.63), channel_id=1, source_target_pairs={{0,4},{1,5},{2,6},{3,7},{4,0},{5,1},{6,2},{7,3},{8,12},{9,13},{10,... | collective-permute-start | bytes 196616 | tf_op jit(solution)/shard_map/ppermute | solution.py:574
  50.4 8.3 %collective-permute-start.8 = (bf16[256,128]{1,0:T(8,128)(2,1)S(1)}, bf16[256,128]{1,0:T(8,128)(2,1)S(1)}, u32[]{:S(2)}, u32[]{:S(2)}) collective-permute-start(bf16[256,128]{1,0:T(8,128)(2,1)S(1)} %get-tuple-element.64), channel_id=1, source_target_pairs={{0,2},{1,3},{2,0},{3,1},{4,6},{5,7},{6,4},{7,5},{8,10},{9,11},{10,... | collective-permute-start | bytes 196616 | tf_op jit(solution)/shard_map/ppermute | solution.py:574
  52.4 7.9 %collective-permute-start.12 = (bf16[256,128]{1,0:T(8,128)(2,1)S(1)}, bf16[256,128]{1,0:T(8,128)(2,1)S(1)}, u32[]{:S(2)}, u32[]{:S(2)}) collective-permute-start(bf16[256,128]{1,0:T(8,128)(2,1)S(1)} %get-tuple-element.71), channel_id=1, source_target_pairs={{0,4},{1,5},{2,6},{3,7},{4,0},{5,1},{6,2},{7,3},{8,12},{9,13},{10,... | collective-permute-start | bytes 196616 | tf_op jit(solution)/shard_map/ppermute | solution.py:574
  58.7 3.5 %collective-permute-start.9 = (bf16[272,128]{1,0:T(8,128)(2,1)S(1)}, bf16[272,128]{1,0:T(8,128)(2,1)S(1)}, u32[]{:S(2)}, u32[]{:S(2)}) collective-permute-start(bf16[272,128]{1,0:T(8,128)(2,1)S(1)} %line_sums_loss.1), channel_id=1, source_target_pairs={{0,1},{1,9},{2,3},{3,11},{4,5},{5,13},{6,7},{7,15},{8,0},{9,8},{10... | collective-permute-start | bytes 208904 | tf_op jit(solution)/shard_map/ppermute | solution.py:434
  60.3 2.8 %collective-permute-start.13 = (bf16[256,128]{1,0:T(8,128)(2,1)S(1)}, bf16[256,128]{1,0:T(8,128)(2,1)S(1)}, u32[]{:S(2)}, u32[]{:S(2)}) collective-permute-start(bf16[256,128]{1,0:T(8,128)(2,1)S(1)} %line_sums.1), channel_id=1, source_target_pairs={{0,1},{1,9},{2,3},{3,11},{4,5},{5,13},{6,7},{7,15},{8,0},{9,8},{10... | collective-permute-start | bytes 196616 | tf_op jit(solution)/shard_map/ppermute | solution.py:434
